TPU v7x, 256 devices: a whole 4x4x8 slice. The times are simulated.
256 devices in a mesh: row: 16 (over z_lo, x, core), col: 16 (over z_hi, y).
Axes of the slice: x: 4, y: 4, z: 8 (z_hi: 4, z_lo: 2; z = z_hi * 2 + z_lo), core: 2. Of those that a mesh axis runs over, the one named last changes fastest.
Arguments:
- gate_pre: bfloat16 [2048, 26624], P('col', 'row'), may hold values from -6 to 6
- up_pre: bfloat16 [2048, 26624], P('col', 'row'), may hold values from -6 to 6
- down_weight: bfloat16 [26624, 16384], P('row', 'col'), may hold values from -0.0390625 to 0.0390625
- out_grad: bfloat16 [2048, 16384], P('row', 'col'), may hold values from -6 to 6
Outputs:
- ffn_out: bfloat16 [2048, 16384], P('row', 'col')
- gate_grad: bfloat16 [2048, 26624], P('col', 'row')
- up_grad: bfloat16 [2048, 26624], P('col', 'row')
All inputs are finite; a program needn't handle non-finite values.
Results may differ from a plain program's by a relative error of at most 0.025.
Values may be sent and summed in bfloat16 or wider, within the bound.
A program may use at most 128 MiB of HBM per device.

v0:
```python
import jax
import jax.numpy as jnp
from jax import lax
from jax.sharding import PartitionSpec as P


def hidden_of(gate_part, up_part):
    gate_value = gate_part.astype(jnp.float32)
    return (jax.nn.silu(gate_value) * up_part.astype(jnp.float32)).astype(jnp.bfloat16)


def local(gate_pre, up_pre, down_weight, out_grad):
    stacked = jnp.stack((gate_pre, up_pre), 0)
    piece = lax.all_gather(stacked, "col", axis=1, tiled=True)
    partial_out = jnp.dot(
        hidden_of(piece[0], piece[1]), down_weight, preferred_element_type=jnp.float32
    )
    ffn_out = lax.psum_scatter(
        partial_out.astype(jnp.bfloat16), "row", scatter_dimension=0, tiled=True
    )
    partial_grad = lax.dot_general(
        lax.all_gather(out_grad, "row", axis=0, tiled=True),
        down_weight,
        (((1,), (1,)), ((), ())),
        preferred_element_type=jnp.float32,
    )
    hidden_grad = lax.psum_scatter(
        partial_grad.astype(jnp.bfloat16), "col", scatter_dimension=0, tiled=True
    ).astype(jnp.float32)
    gate_value = gate_pre.astype(jnp.float32)
    up_value = up_pre.astype(jnp.float32)
    sigma = jax.nn.sigmoid(gate_value)
    gate_grad = (hidden_grad * up_value * sigma * (1.0 + gate_value * (1.0 - sigma))).astype(
        jnp.bfloat16
    )
    up_grad = (hidden_grad * gate_value * sigma).astype(jnp.bfloat16)
    return (ffn_out, gate_grad, up_grad)


def solution(mesh):
    return jax.shard_map(
        local,
        mesh=mesh,
        in_specs=(P("col", "row"), P("col", "row"), P("row", "col"), P("row", "col")),
        out_specs=(P("row", "col"), P("col", "row"), P("col", "row")),
        check_vma=False,
    )
```

profile of v0, /device:TPU:1, one launch (start us, length us, event | category | flops | bytes accessed | tf_op | source)
XLA Modules:
  0.0 416.2 jit_solution(5023489437076894196)
XLA Ops:
  7.2 0.0 copy-start
  7.2 0.0 all-gather.5.cloned.1.call-start
  7.2 0.7 all-gather.5.cloned.1.call-update
  7.9 0.0 all-gather.3.cloned.1.call-start
  8.0 2.5 pad_maximum_fusion
  10.4 0.0 all-gather.3.cloned.1.call-update
  10.5 0.0 reduce-scatter.5.cloned.1.call-start
  10.5 43.6 %all-gather.5.cloned.1.call-done = bf16[2048,1024]{1,0:T(8,128)(2,1)} async-done(((bf16[128,1024]{1,0:T(8,128)(2,1)}), bf16[2048,1024]{1,0:T(8,128)(2,1)}) %all-gather.5.cloned.1.call-update) | async-done | bytes 4194320 | tf_op jit(solution)/shard_map/all_gather | solution.py:22
  54.1 0.0 copy-done
  54.1 11.3 %convolution_convert_fusion = bf16[2048,1664]{1,0:T(8,128)(2,1)} fusion(bf16[2048,1024]{1,0:T(8,128)(2,1)} %all-gather.5.cloned.1.call-done, bf16[1664,1024]{1,0:T(8,128)(2,1)S(1)} %copy-done), kind=kOutput, calls=%fused_computation.7 | convolution fusion | flops 6982729728 | bytes 14417920 | tf_op jit(solution)/shard_map/dot_general | solution.py:21
  65.4 0.0 reduce-scatter.5.cloned.1.call-update
  65.5 0.0 reduce-scatter.3.cloned.1.call-start
  65.5 154.6 %all-gather.3.cloned.1.call-done = bf16[2,2048,1664]{2,1,0:T(8,128)(2,1)} async-done(((bf16[2,128,1664]{2,1,0:T(8,128)(2,1)}), bf16[2,2048,1664]{2,1,0:T(8,128)(2,1)}) %all-gather.3.cloned.1.call-update) | async-done | bytes 13631504 | tf_op jit(solution)/shard_map/all_gather | solution.py:14
  220.1 13.0 %fusion.7 = bf16[2048,1024]{1,0:T(8,128)(2,1)} fusion(bf16[1664,1024]{1,0:T(8,128)(2,1)S(1)} %copy-done, bf16[2,2048,1664]{2,1,0:T(8,128)(2,1)} %all-gather.3.cloned.1.call-done), kind=kOutput, calls=%fused_computation.11 | convolution fusion | flops 7008681984 | bytes 21233664 | tf_op jit(solution)/shard_map/dot_general | solution.py:15
  233.1 0.0 reduce-scatter.3.cloned.1.call-update
  233.2 107.5 %reduce-scatter.5.cloned.1.call-done = bf16[128,1664]{1,0:T(8,128)(2,1)} async-done(((bf16[2048,1664]{1,0:T(8,128)(2,1)}), bf16[128,1664]{1,0:T(8,128)(2,1)}) %reduce-scatter.5.cloned.1.call-update) | async-done | bytes 426000 | tf_op jit(solution)/shard_map/reduce_scatter | solution.py:27
  340.6 2.6 fusion.18
  343.2 66.4 %reduce-scatter.3.cloned.1.call-done = bf16[128,1024]{1,0:T(8,128)(2,1)} async-done(((bf16[2048,1024]{1,0:T(8,128)(2,1)}), bf16[128,1024]{1,0:T(8,128)(2,1)}) %reduce-scatter.3.cloned.1.call-update) | async-done | bytes 262160 | tf_op jit(solution)/shard_map/reduce_scatter | solution.py:18
Async XLA Ops:
  7.2 47.0 %copy-start = (bf16[1664,1024]{1,0:T(8,128)(2,1)S(1)}, bf16[1664,1024]{1,0:T(8,128)(2,1)}, u32[]{:S(2)}) copy-start(bf16[1664,1024]{1,0:T(8,128)(2,1)} %param.6) | copy-start | bytes 10223620
  7.2 47.0 %all-gather.5.cloned.1.call-start = ((), (), s32[]{:S(2)}) async-start(), calls=%async_computation.4 | async-start | bytes 4456448 | tf_op jit(solution)/shard_map/all_gather | solution.py:22
  7.9 212.2 %all-gather.3.cloned.1.call-start = ((), (), s32[]{:S(2)}) async-start(), calls=%async_computation.2 | async-start | bytes 14483456 | tf_op jit(solution)/shard_map/all_gather | solution.py:14
  10.5 330.2 %reduce-scatter.5.cloned.1.call-start = ((), (), s32[]{:S(2)}) async-start(), calls=%async_computation.5 | async-start | bytes 7241728 | tf_op jit(solution)/shard_map/reduce_scatter | solution.py:27
  65.5 344.2 %reduce-scatter.3.cloned.1.call-start = ((), (), s32[]{:S(2)}) async-start(), calls=%async_computation.3 | async-start | bytes 4456448 | tf_op jit(solution)/shard_map/reduce_scatter | solution.py:18
Sparse Core Ops, SparseCore 0:
  9.9 44.2 all-gather.4
  56.6 163.4 all-gather.2
  223.9 116.7 reduce-scatter.4
  343.8 65.8 reduce-scatter.2
where the time goes:
time: 419 us; the launch traced here: 416 us
  waiting for transfers between devices  373 us (89%)
  matrix products  24.3 us (6%)
  between operations  13.8 us (3%)
  other arithmetic  5.09 us (1%)
    all_gather x1, waiting for transfers between devices, local(): piece = lax.all_gather(stacked, 'col', axis=1, tiled=True)  155 us
    reduce_scatter x1, waiting for transfers between devices, local(): lax.psum_scatter(partial_grad.astype(jnp.bfloat16), 'col', scatter_dimens...  107 us
    reduce_scatter x1, waiting for transfers between devices, local(): lax.psum_scatter(partial_out.astype(jnp.bfloat16), 'row', scatter_dimensi...  66.4 us
    all_gather x1, waiting for transfers between devices, local(): lax.all_gather(out_grad, 'row', axis=0, tiled=True)  43.6 us
    dot_general x1, matrix products, local(): jnp.dot(hidden_of(piece[0], piece[1]), down_weight, preferred_element_typ...  13 us
    dot_general x1, matrix products, local(): lax.dot_general(lax.all_gather(out_grad, 'row', axis=0, tiled=True), down...  11.3 us
  transfers between devices with their start and end apart: 4, of which 4 were waited for; matrix products, arithmetic and copies ran while one was open for 7% of the time, Pallas kernels for 0%

commit v1 on v0

--- a/solution.py
+++ b/solution.py
@@ -10,11 +10,8 @@
 
 
 def local(gate_pre, up_pre, down_weight, out_grad):
-    stacked = jnp.stack((gate_pre, up_pre), 0)
-    piece = lax.all_gather(stacked, "col", axis=1, tiled=True)
-    partial_out = jnp.dot(
-        hidden_of(piece[0], piece[1]), down_weight, preferred_element_type=jnp.float32
-    )
+    hidden = lax.all_gather(hidden_of(gate_pre, up_pre), "col", axis=0, tiled=True)
+    partial_out = jnp.dot(hidden, down_weight, preferred_element_type=jnp.float32)
     ffn_out = lax.psum_scatter(
         partial_out.astype(jnp.bfloat16), "row", scatter_dimension=0, tiled=True
     )

time: 419 us -> 368 us (0.88)
  waiting for transfers between devices: 373 us -> 325 us
    all_gather x1, waiting for transfers between devices: 155 us -> 94 us  [local(): lax.all_gather(hidden_of(gate_pre, up_pre), 'col', axis=0, tiled=True)]
    reduce_scatter x1, waiting for transfers between devices: 66.4 us -> 72.4 us  [local(): lax.psum_scatter(partial_out.astype(jnp.bfloat16), 'row', scatter_dimensi...]
    reduce_scatter x1, waiting for transfers between devices: 107 us -> 112 us  [local(): lax.psum_scatter(partial_grad.astype(jnp.bfloat16), 'col', scatter_dimens...]
  transfers between devices with their start and end apart: 4 -> 4, of which waited for: 4 -> 4; matrix products, arithmetic and copies ran while one was open for 7% -> 0% of each run, Pallas kernels for 0% -> 0%
where the time goes in v1:
time: 368 us; the launch traced here: 365 us
  waiting for transfers between devices  325 us (88%)
  matrix products  22.6 us (6%)
  between operations  13.8 us (4%)
    reduce_scatter x1, waiting for transfers between devices, local(): lax.psum_scatter(partial_grad.astype(jnp.bfloat16), 'col', scatter_dimens...  112 us
    all_gather x1, waiting for transfers between devices, local(): lax.all_gather(hidden_of(gate_pre, up_pre), 'col', axis=0, tiled=True)  94 us
    reduce_scatter x1, waiting for transfers between devices, local(): lax.psum_scatter(partial_out.astype(jnp.bfloat16), 'row', scatter_dimensi...  72.4 us
    all_gather x1, waiting for transfers between devices, local(): lax.all_gather(out_grad, 'row', axis=0, tiled=True)  46.2 us
    dot_general x1, matrix products, local(): lax.dot_general(lax.all_gather(out_grad, 'row', axis=0, tiled=True), down...  11.4 us
    dot_general x1, matrix products, local(): jnp.dot(hidden, down_weight, preferred_element_type=jnp.float32)  11.2 us
  transfers between devices with their start and end apart: 4, of which 4 were waited for; matrix products, arithmetic and copies ran while one was open for 0% of the time, Pallas kernels for 0%

profile of v1, /device:TPU:1, one launch (start us, length us, event | category | flops | bytes accessed | tf_op | source)
XLA Modules:
  0.0 364.8 jit_solution(15161742043120903655)
XLA Ops:
  7.2 0.0 copy-start
  7.2 0.0 all-gather.5.cloned.1.call-start
  7.2 0.7 all-gather.5.cloned.1.call-update
  7.9 0.0 reduce-scatter.5.cloned.1.call-start
  8.0 46.2 %all-gather.5.cloned.1.call-done = bf16[2048,1024]{1,0:T(8,128)(2,1)} async-done(((bf16[128,1024]{1,0:T(8,128)(2,1)}), bf16[2048,1024]{1,0:T(8,128)(2,1)}) %all-gather.5.cloned.1.call-update) | async-done | bytes 4194320 | tf_op jit(solution)/shard_map/all_gather | solution.py:19
  54.1 0.0 copy-done
  54.1 11.4 %convolution_convert_fusion = bf16[2048,1664]{1,0:T(8,128)(2,1)} fusion(bf16[2048,1024]{1,0:T(8,128)(2,1)} %all-gather.5.cloned.1.call-done, bf16[1664,1024]{1,0:T(8,128)(2,1)S(1)} %copy-done), kind=kOutput, calls=%fused_computation | convolution fusion | flops 6982729728 | bytes 14417920 | tf_op jit(solution)/shard_map/dot_general | solution.py:18
  65.5 0.0 reduce-scatter.5.cloned.1.call-update
  65.5 0.0 all-gather.3.cloned.1.call-start
  65.6 112.2 %reduce-scatter.5.cloned.1.call-done = bf16[128,1664]{1,0:T(8,128)(2,1)} async-done(((bf16[2048,1664]{1,0:T(8,128)(2,1)}), bf16[128,1664]{1,0:T(8,128)(2,1)}) %reduce-scatter.5.cloned.1.call-update) | async-done | bytes 426000 | tf_op jit(solution)/shard_map/reduce_scatter | solution.py:24
  177.8 2.8 fusion.9
  180.5 0.0 all-gather.3.cloned.1.call-update
  180.6 0.0 reduce-scatter.3.cloned.1.call-start
  180.6 94.0 %all-gather.3.cloned.1.call-done = bf16[2048,1664]{1,0:T(8,128)(2,1)} async-done(((bf16[128,1664]{1,0:T(8,128)(2,1)}), bf16[2048,1664]{1,0:T(8,128)(2,1)}) %all-gather.3.cloned.1.call-update) | async-done | bytes 6815760 | tf_op jit(solution)/shard_map/all_gather | solution.py:13
  274.6 11.2 %convolution_convert_fusion.1 = bf16[2048,1024]{1,0:T(8,128)(2,1)} fusion(bf16[2048,1664]{1,0:T(8,128)(2,1)} %all-gather.3.cloned.1.call-done, bf16[1664,1024]{1,0:T(8,128)(2,1)S(1)} %copy-done), kind=kOutput, calls=%fused_computation.1 | convolution fusion | flops 6981419008 | bytes 14417920 | tf_op jit(solution)/shard_map/dot_general | solution.py:14
  285.9 0.0 reduce-scatter.3.cloned.1.call-update
  285.9 72.4 %reduce-scatter.3.cloned.1.call-done = bf16[128,1024]{1,0:T(8,128)(2,1)} async-done(((bf16[2048,1024]{1,0:T(8,128)(2,1)}), bf16[128,1024]{1,0:T(8,128)(2,1)}) %reduce-scatter.3.cloned.1.call-update) | async-done | bytes 262160 | tf_op jit(solution)/shard_map/reduce_scatter | solution.py:15
Async XLA Ops:
  7.2 47.0 %copy-start = (bf16[1664,1024]{1,0:T(8,128)(2,1)S(1)}, bf16[1664,1024]{1,0:T(8,128)(2,1)}, u32[]{:S(2)}) copy-start(bf16[1664,1024]{1,0:T(8,128)(2,1)} %param.6) | copy-start | bytes 10223620
  7.2 47.0 %all-gather.5.cloned.1.call-start = ((), (), s32[]{:S(2)}) async-start(), calls=%async_computation.4 | async-start | bytes 4456448 | tf_op jit(solution)/shard_map/all_gather | solution.py:19
  7.9 169.8 %reduce-scatter.5.cloned.1.call-start = ((), (), s32[]{:S(2)}) async-start(), calls=%async_computation.5 | async-start | bytes 7241728 | tf_op jit(solution)/shard_map/reduce_scatter | solution.py:24
  65.5 209.1 %all-gather.3.cloned.1.call-start = ((), (), s32[]{:S(2)}) async-start(), calls=%async_computation.2 | async-start | bytes 7241728 | tf_op jit(solution)/shard_map/all_gather | solution.py:13
  180.6 177.7 %reduce-scatter.3.cloned.1.call-start = ((), (), s32[]{:S(2)}) async-start(), calls=%async_computation.3 | async-start | bytes 4456448 | tf_op jit(solution)/shard_map/reduce_scatter | solution.py:15
Sparse Core Ops, SparseCore 0:
  9.9 44.2 all-gather.4
  65.7 112.0 reduce-scatter.4
  180.7 93.8 all-gather.2
  286.0 72.1 reduce-scatter.2

commit v2 on v1

v2 whole, which is shorter than its diff:
```python
import functools

import jax
import jax.numpy as jnp
from jax import lax
from jax.experimental import pallas as pl
from jax.experimental.pallas import tpu as pltpu
from jax.sharding import PartitionSpec as P

BF16, F32 = jnp.bfloat16, jnp.float32

Z_FIRST = 1408

MESSAGES = (
    ["g_z"]
    + [f"g_{what}{k}" for k in range(2) for what in ("xp", "xm", "hp", "hm", "s", "sp", "sm", "sf")]
    + ["h_zp", "h_zm", "h_zhp", "h_zhm", "q_yp", "q_ym", "q_yhp", "q_yhm", "q_zp", "q_zm", "q_zhp", "q_zhm"]
    + [f"h_{what}{k}" for k in range(4) for what in ("yp", "ym", "yhp", "yhm")]
    + [f"p_{what}{k}" for k in range(4) for what in ("yp", "ym", "yhp", "yhm")]
    + ["p_zp", "p_zm", "p_zhp", "p_zhm", "r_yp", "r_ym", "r_yhp", "r_yhm", "r_zp", "r_zm", "r_zhp", "r_zhm"]
    + [f"o_d{k}" for k in range(4)]
    + [f"o_{what}{m}" for m in range(2) for what in ("xp", "xm", "hp", "hm")]
    + ["o_z"]
)
NUMBER = {name: number for number, name in enumerate(MESSAGES)}


def kernel(
    gate, up, weight, cot, out, gate_grad, up_grad,
    hid, cots, part_out, part_grad,
    from_sib, x_full, x_half, x_sum, zl_in,
    y_full, y_half, y_sum, z_full, z_half,
    qz_full, qz_half, q_sum, qy_full, qy_half,
    send_sems, recv_sems,
):
    tokens, units = gate.shape
    feats = cot.shape[1]
    half = tokens // 2
    A, B, ALL = pl.ds(0, half), pl.ds(half, half), pl.ds(0, tokens)
    first = Z_FIRST
    FIRST, REST = pl.ds(0, first), pl.ds(first, units - first)

    row, col = lax.axis_index("row"), lax.axis_index("col")
    zl, x, core = row // 8, (row // 2) % 4, row % 2
    z, y = col // 4, col % 4
    xp, xm, xf = (x + 1) % 4, (x + 3) % 4, (x + 2) % 4
    yp, ym, yf = (y + 1) % 4, (y + 3) % 4, (y + 2) % 4
    zp, zm, zf = (z + 1) % 4, (z + 3) % 4, (z + 2) % 4

    def at_row(zl_, x_, core_):
        return zl_ * 8 + x_ * 2 + core_

    def at_col(z_, y_):
        return z_ * 4 + y_

    near = {
        "xp": {"row": at_row(zl, xp, core)},
        "xm": {"row": at_row(zl, xm, core)},
        "zl": {"row": at_row(1 - zl, x, core)},
        "sib": {"row": at_row(zl, x, 1 - core)},
        "yp": {"col": at_col(z, yp)},
        "ym": {"col": at_col(z, ym)},
        "zp": {"col": at_col(zp, y)},
        "zm": {"col": at_col(zm, y)},
    }

    sent = []

    def copy(name, src, dst, to):
        number = NUMBER[name]
        return pltpu.make_async_remote_copy(
            src_ref=src,
            dst_ref=dst,
            send_sem=send_sems.at[number],
            recv_sem=recv_sems.at[number],
            device_id=near[to],
            device_id_type=pl.DeviceIdType.MESH,
        )

    def send(name, src, dst, to):
        one = copy(name, src, dst, to)
        one.start()
        sent.append(one)

    def arrived(name, ref):
        copy(name, ref, ref, "sib").wait_recv()

    def chunks(count, body):
        def step(i, carry):
            body(pl.ds(pl.multiple_of(i * 16, 16), 16))
            return carry

        lax.fori_loop(0, count // 16, step, 0)

    def wide(ref):
        return ref[...].astype(F32)

    def add_into(ref, other):
        lead = (slice(None),) * (len(ref.shape) - 2)

        def body(rows):
            index = lead + (rows,)
            ref[index] = (ref[index].astype(F32) + other[index].astype(F32)).astype(BF16)

        chunks(ref.shape[-2], body)

    def sum_to(ref, terms):
        lead = (slice(None),) * (len(ref.shape) - 2)

        def body(rows):
            index = lead + (rows,)
            total = terms[0][index].astype(F32)
            for term in terms[1:]:
                total = total + term[index].astype(F32)
            ref[index] = total.astype(BF16)

        chunks(ref.shape[-2], body)

    barrier = pltpu.get_barrier_semaphore()
    for to in near.values():
        pl.semaphore_signal(barrier, inc=1, device_id=to, device_id_type=pl.DeviceIdType.MESH)

    cots[row] = cot[...]

    def make_hidden(rows):
        value = gate[rows].astype(F32)
        silu = value / (1.0 + jnp.exp(-value))
        hid[col, rows] = (silu * up[rows].astype(F32)).astype(BF16)

    chunks(tokens, make_hidden)
    pl.semaphore_wait(barrier, len(near))

    zls = (zl, 1 - zl)

    def g_block(k, x_, core_=core):
        return cots.at[at_row(zls[k], x_, core_)]

    def g_spread(k):
        send(f"g_xp{k}", g_block(k, x), g_block(k, x), "xp")
        send(f"g_xm{k}", g_block(k, x), g_block(k, x), "xm")
        send(f"g_s{k}", g_block(k, x), g_block(k, x), "sib")

    def g_relay(k):
        arrived(f"g_xp{k}", g_block(k, xm))
        send(f"g_hp{k}", g_block(k, xm).at[A], g_block(k, xm).at[A], "xp")
        arrived(f"g_xm{k}", g_block(k, xp))
        send(f"g_hm{k}", g_block(k, xp).at[B], g_block(k, xp).at[B], "xm")
        send(f"g_sm{k}", g_block(k, xm), g_block(k, xm), "sib")
        send(f"g_sp{k}", g_block(k, xp), g_block(k, xp), "sib")

    def g_far(k):
        arrived(f"g_hp{k}", g_block(k, xf).at[A])
        arrived(f"g_hm{k}", g_block(k, xf).at[B])
        send(f"g_sf{k}", g_block(k, xf), g_block(k, xf), "sib")

    def g_end(k):
        for what, x_ in (("s", x), ("sm", xm), ("sp", xp), ("sf", xf)):
            arrived(f"g_{what}{k}", g_block(k, x_, 1 - core))

    zs = (z, zm, zp, zf)

    def h_block(z_, y_, rows=ALL):
        return hid.at[at_col(z_, y_), rows, FIRST]

    def q_block(y_, rows=ALL):
        return hid.at[at_col(z, y_), rows, REST]

    def q_four(z_, rows=ALL):
        return hid.at[pl.ds(z_ * 4, 4), rows, REST]

    def h_spread(k):
        block = h_block(zs[k], y)
        send(f"h_yp{k}", block, block, "yp")
        send(f"h_ym{k}", block, block, "ym")

    def h_relay(k):
        arrived(f"h_yp{k}", h_block(zs[k], ym))
        block = h_block(zs[k], ym, A)
        send(f"h_yhp{k}", block, block, "yp")
        arrived(f"h_ym{k}", h_block(zs[k], yp))
        block = h_block(zs[k], yp, B)
        send(f"h_yhm{k}", block, block, "ym")

    def h_far(k):
        arrived(f"h_yhp{k}", h_block(zs[k], yf, A))
        arrived(f"h_yhm{k}", h_block(zs[k], yf, B))

    def q_y_relay():
        arrived("q_yp", q_block(ym))
        send("q_yhp", q_block(ym, A), q_block(ym, A), "yp")
        arrived("q_ym", q_block(yp))
        send("q_yhm", q_block(yp, B), q_block(yp, B), "ym")

    def q_z_spread():
        arrived("q_yhp", q_block(yf, A))
        arrived("q_yhm", q_block(yf, B))
        send("q_zp", q_four(z), q_four(z), "zp")
        send("q_zm", q_four(z), q_four(z), "zm")

    def h_z_relay():
        arrived("h_zp", h_block(zm, y))
        send("h_zhp", h_block(zm, y, A), h_block(zm, y, A), "zp")
        arrived("h_zm", h_block(zp, y))
        send("h_zhm", h_block(zp, y, B), h_block(zp, y, B), "zm")

    def q_z_relay():
        arrived("q_zp", q_four(zm))
        send("q_zhp", q_four(zm, A), q_four(zm, A), "zp")
        arrived("q_zm", q_four(zp))
        send("q_zhm", q_four(zp, B), q_four(zp, B), "zm")

    def q_z_far():
        arrived("q_zhp", q_four(zf, A))
        arrived("q_zhm", q_four(zf, B))

    def backward(z_):
        four = pl.ds(z_ * 4, 4)

        def tile(start, width):
            left = cots[four].reshape(4 * tokens, feats)
            product = lax.dot_general(
                left, weight[pl.ds(start, width)], (((1,), (1,)), ((), ())), preferred_element_type=F32
            )
            part_grad[four, :, pl.ds(start, width)] = product.astype(BF16).reshape(4, tokens, width)

        def step(i, carry):
            tile(pl.multiple_of(i * 256, 256), 256)
            return carry

        lax.fori_loop(0, units // 256, step, 0)
        if units % 256:
            tile(units // 256 * 256, units % 256)

    def forward(z_):
        four = pl.ds(z_ * 4, 4)

        def step(i, carry):
            columns = pl.ds(pl.multiple_of(i * 256, 256), 256)
            left = hid[four].reshape(4 * tokens, units)
            product = jnp.dot(left, weight[:, columns], preferred_element_type=F32).astype(BF16)
            for j in range(4):
                part_out[j % 2, z_ * 2 + j // 2, :, columns] = product[j * tokens : (j + 1) * tokens]
            return carry

        lax.fori_loop(0, feats // 256, step, 0)

    def pg(z_, y_, rows=ALL):
        return part_grad.at[at_col(z_, y_), rows, FIRST]

    def pq(z_, rows=ALL):
        return part_grad.at[pl.ds(z_ * 4, 4), rows, REST]

    def p_start(k):
        send(f"p_yhp{k}", pg(zs[k], yf, A), y_half.at[0, k], "yp")
        send(f"p_yhm{k}", pg(zs[k], yf, B), y_half.at[1, k], "ym")

    def p_relay(k):
        arrived(f"p_yhp{k}", y_half.at[0, k])
        add_into(pg(zs[k], yp, A), y_half.at[0, k])
        send(f"p_yp{k}", pg(zs[k], yp), y_full.at[0, k], "yp")
        arrived(f"p_yhm{k}", y_half.at[1, k])
        add_into(pg(zs[k], ym, B), y_half.at[1, k])
        send(f"p_ym{k}", pg(zs[k], ym), y_full.at[1, k], "ym")

    def p_here(k):
        arrived(f"p_yp{k}", y_full.at[0, k])
        arrived(f"p_ym{k}", y_full.at[1, k])
        if k:
            sum_to(y_sum.at[k - 1], (pg(zs[k], y), y_full.at[0, k], y_full.at[1, k]))

    def p_z_start():
        send("p_zhp", y_sum.at[2, A], z_half.at[0], "zp")
        send("p_zhm", y_sum.at[2, B], z_half.at[1], "zm")

    def p_z_relay():
        arrived("p_zhp", z_half.at[0])
        add_into(y_sum.at[1, A], z_half.at[0])
        send("p_zp", y_sum.at[1], z_full.at[0], "zp")
        arrived("p_zhm", z_half.at[1])
        add_into(y_sum.at[0, B], z_half.at[1])
        send("p_zm", y_sum.at[0], z_full.at[1], "zm")

    def r_z_start():
        send("r_zhp", pq(zf, A), qz_half.at[0], "zp")
        send("r_zhm", pq(zf, B), qz_half.at[1], "zm")

    def r_z_relay():
        arrived("r_zhp", qz_half.at[0])
        add_into(pq(zp, A), qz_half.at[0])
        send("r_zp", pq(zp), qz_full.at[0], "zp")
        arrived("r_zhm", qz_half.at[1])
        add_into(pq(zm, B), qz_half.at[1])
        send("r_zm", pq(zm), qz_full.at[1], "zm")

    def r_y_start():
        arrived("r_zp", qz_full.at[0])
        arrived("r_zm", qz_full.at[1])
        sum_to(q_sum, (pq(z), qz_full.at[0], qz_full.at[1]))
        send("r_yhp", q_sum.at[yf, A], qy_half.at[0], "yp")
        send("r_yhm", q_sum.at[yf, B], qy_half.at[1], "ym")

    def r_y_relay():
        arrived("r_yhp", qy_half.at[0])
        add_into(q_sum.at[yp, A], qy_half.at[0])
        send("r_yp", q_sum.at[yp], qy_full.at[0], "yp")
        arrived("r_yhm", qy_half.at[1])
        add_into(q_sum.at[ym, B], qy_half.at[1])
        send("r_ym", q_sum.at[ym], qy_full.at[1], "ym")

    def o_swap(k, z_):
        chips = pl.ds(z_ * 2, 2)
        send(f"o_d{k}", part_out.at[1 - core, chips], from_sib.at[chips], "sib")

    def o_pair(k, z_):
        chips = pl.ds(z_ * 2, 2)
        arrived(f"o_d{k}", from_sib.at[chips])
        add_into(part_out.at[core, chips], from_sib.at[chips])

    o_zls = (z // 2, 1 - z // 2)

    def o_block(m, x_, rows=ALL):
        return part_out.at[core, o_zls[m] * 4 + x_, rows]

    def o_start(m):
        send(f"o_hp{m}", o_block(m, xf, A), x_half.at[0, m], "xp")
        send(f"o_hm{m}", o_block(m, xf, B), x_half.at[1, m], "xm")

    def o_relay(m):
        arrived(f"o_hp{m}", x_half.at[0, m])
        add_into(o_block(m, xp, A), x_half.at[0, m])
        send(f"o_xp{m}", o_block(m, xp), x_full.at[0, m], "xp")
        arrived(f"o_hm{m}", x_half.at[1, m])
        add_into(o_block(m, xm, B), x_half.at[1, m])
        send(f"o_xm{m}", o_block(m, xm), x_full.at[1, m], "xm")

    def o_here(m):
        arrived(f"o_xp{m}", x_full.at[0, m])
        arrived(f"o_xm{m}", x_full.at[1, m])
        sum_to(x_sum.at[o_zls[m]], (o_block(m, x), x_full.at[0, m], x_full.at[1, m]))

    def o_end():
        arrived("o_z", zl_in)

        def body(rows):
            out[rows] = (x_sum[zl, rows].astype(F32) + zl_in[rows].astype(F32)).astype(BF16)

        chunks(tokens, body)

    send("g_z", g_block(0, x), g_block(0, x), "zl")
    g_spread(0)
    send("q_yp", q_block(y), q_block(y), "yp")
    send("q_ym", q_block(y), q_block(y), "ym")
    send("h_zp", h_block(z, y), h_block(z, y), "zp")
    send("h_zm", h_block(z, y), h_block(z, y), "zm")
    h_spread(0)
    q_y_relay()
    arrived("g_z", g_block(1, x))
    g_spread(1)
    g_relay(0)
    q_z_spread()
    h_relay(0)
    h_z_relay()
    h_spread(1)
    h_spread(2)
    g_relay(1)
    g_far(0)
    h_far(0)
    g_far(1)
    g_end(0)
    g_end(1)
    backward(zf)
    p_start(3)
    q_z_relay()
    arrived("h_zhp", h_block(zf, y, A))
    arrived("h_zhm", h_block(zf, y, B))
    h_spread(3)
    h_relay(1)
    h_relay(2)
    backward(zm)
    p_start(1)
    p_relay(3)
    backward(zp)
    p_start(2)
    r_z_start()
    h_relay(3)
    backward(z)
    p_start(0)
    p_relay(1)
    p_relay(2)
    p_here(3)
    p_z_start()
    p_relay(0)
    r_z_relay()
    q_z_far()
    forward(z)
    o_swap(0, z)
    h_far(1)
    h_far(2)
    pair = z + 1 - 2 * (z % 2)
    other = zp + zm - pair
    forward(pair)
    o_swap(1, pair)
    o_pair(0, z)
    forward(other)
    o_swap(2, other)
    o_pair(1, pair)
    o_start(0)
    h_far(3)
    forward(zf)
    o_swap(3, zf)
    o_pair(2, other)
    o_relay(0)
    p_here(1)
    p_here(2)
    p_z_relay()
    o_pair(3, zf)
    o_start(1)
    r_y_start()
    o_here(0)
    o_relay(1)
    r_y_relay()
    o_here(1)
    send("o_z", x_sum.at[1 - zl], zl_in, "zl")
    p_here(0)
    o_end()
    arrived("p_zp", z_full.at[0])
    arrived("p_zm", z_full.at[1])
    arrived("r_yp", qy_full.at[0])
    arrived("r_ym", qy_full.at[1])

    def finish(rows, columns, terms):
        grad = terms[0].astype(F32)
        for term in terms[1:]:
            grad = grad + term.astype(F32)
        gate_value = gate[rows, columns].astype(F32)
        up_value = up[rows, columns].astype(F32)
        sigma = 1.0 / (1.0 + jnp.exp(-gate_value))
        scaled = grad * sigma
        gate_grad[rows, columns] = (scaled * up_value * (1.0 + gate_value * (1.0 - sigma))).astype(BF16)
        up_grad[rows, columns] = (scaled * gate_value).astype(BF16)

    def last(rows):
        finish(
            rows,
            FIRST,
            (
                part_grad[col, rows, FIRST],
                y_full[0, 0, rows],
                y_full[1, 0, rows],
                z_full[0, rows],
                z_full[1, rows],
            ),
        )
        finish(rows, REST, (q_sum[y, rows], qy_full[0, rows], qy_full[1, rows]))

    chunks(tokens, last)
    for one in sent:
        one.wait_send()


def local(gate_pre, up_pre, down_weight, out_grad):
    tokens, units = gate_pre.shape
    feats = out_grad.shape[1]
    first, rest, half = Z_FIRST, units - Z_FIRST, tokens // 2

    def vmem(*shape):
        return pltpu.VMEM(shape, BF16)

    whole = pl.BlockSpec(memory_space=pltpu.VMEM)
    return pl.pallas_call(
        kernel,
        out_shape=(
            jax.ShapeDtypeStruct((tokens, feats), BF16),
            jax.ShapeDtypeStruct((tokens, units), BF16),
            jax.ShapeDtypeStruct((tokens, units), BF16),
        ),
        in_specs=[whole] * 4,
        out_specs=(whole,) * 3,
        scratch_shapes=[
            vmem(16, tokens, units),
            vmem(16, tokens, feats),
            vmem(2, 8, tokens, feats),
            vmem(16, tokens, units),
            vmem(8, tokens, feats),
            vmem(2, 2, tokens, feats),
            vmem(2, 2, half, feats),
            vmem(2, tokens, feats),
            vmem(tokens, feats),
            vmem(2, 4, tokens, first),
            vmem(2, 4, half, first),
            vmem(3, tokens, first),
            vmem(2, tokens, first),
            vmem(2, half, first),
            vmem(2, 4, tokens, rest),
            vmem(2, 4, half, rest),
            vmem(4, tokens, rest),
            vmem(2, tokens, rest),
            vmem(2, half, rest),
            pltpu.SemaphoreType.DMA((len(MESSAGES),)),
            pltpu.SemaphoreType.DMA((len(MESSAGES),)),
        ],
        compiler_params=pltpu.CompilerParams(
            collective_id=0, has_side_effects=True, vmem_limit_bytes=60 * 1024 * 1024
        ),
        cost_estimate=pl.CostEstimate(
            flops=4 * 16 * tokens * units * feats, bytes_accessed=8 * 1024 * 1024, transcendentals=0
        ),
    )(gate_pre, up_pre, down_weight, out_grad)


def solution(mesh):
    return jax.shard_map(
        local,
        mesh=mesh,
        in_specs=(P("col", "row"), P("col", "row"), P("row", "col"), P("row", "col")),
        out_specs=(P("row", "col"), P("col", "row"), P("col", "row")),
        check_vma=False,
    )
```

time: 368 us -> 143 us (0.39)
  waiting for transfers between devices: 325 us -> 0 us
  Pallas kernels: 0 us -> 137 us
  matrix products: 22.6 us -> 0 us
  between operations: 13.8 us -> 0.64 us
  local copies, waits for them, and re-layouts: 0.01 us -> 5.26 us
    reduce_scatter x2 -> x0, waiting for transfers between devices: 185 us -> none  [the longest x1 112 us: local(): lax.psum_scatter(partial_grad.astype(jnp.bfloat16), 'col', scatter_dimens...]
    all_gather x2 -> x0, waiting for transfers between devices: 140 us -> none  [the longest x1 94 us: local(): lax.all_gather(hidden_of(gate_pre, up_pre), 'col', axis=0, tiled=True)]
    pallas_call x0 -> x1, Pallas kernels: none -> 137 us  [local(): pl.pallas_call(kernel, out_shape=(jax.ShapeDtypeStruct((tokens, feats), B...]
    dot_general x2 -> x0, matrix products: 22.6 us -> none  [the longest x1 11.4 us: local(): lax.dot_general(lax.all_gather(out_grad, 'row', axis=0, tiled=True), down...]
    unnamed x2 -> x3, local copies, waits for them, and re-layouts: 0.01 us -> 5.26 us
  transfers between devices with their start and end apart: 4 -> 0, of which waited for: 4 -> 0; matrix products, arithmetic and copies ran while one was open for 0% -> 0% of each run, Pallas kernels for 0% -> 0%
where the time goes in v2:
time: 143 us
  Pallas kernels  137 us (96%)
  local copies, waits for them, and re-layouts  5.26 us (4%)
    pallas_call x1, Pallas kernels, local(): pl.pallas_call(kernel, out_shape=(jax.ShapeDtypeStruct((tokens, feats), B...  137 us
    unnamed x3, local copies, waits for them, and re-layouts  5.26 us

profile of v2, /device:TPU:1, one launch (start us, length us, event | category | flops | bytes accessed | tf_op | source)
XLA Modules:
  0.0 143.0 jit_solution(4705436224459991493)
XLA Ops:
  0.6 137.1 %shard_map.67 = (bf16[128,1024]{1,0:T(8,128)(2,1)}, bf16[128,1664]{1,0:T(8,128)(2,1)}, bf16[128,1664]{1,0:T(8,128)(2,1)}) custom-call(bf16[128,1664]{1,0:T(8,128)(2,1)} %gate.1, bf16[128,1664]{1,0:T(8,128)(2,1)} %up.1, bf16[1664,1024]{1,0:T(8,128)(2,1)} %weight.1, bf16[128,1024]{1,0:T(8,128)(2,1)} %cot.1), custom_call_target="tpu_custom_call" | custom-call | flops 13958643712 | bytes 8388608 | tf_op jit(solution)/shard_map/pallas_call | solution.py:470
  137.8 1.7 %copy.10 = bf16[128,1024]{1,0:T(8,128)(2,1)} copy(bf16[128,1024]{1,0:T(8,128)(2,1)} %get-tuple-element.6) | data formatting | bytes 524288
  139.4 1.8 %copy.11 = bf16[128,1664]{1,0:T(8,128)(2,1)} copy(bf16[128,1664]{1,0:T(8,128)(2,1)} %get-tuple-element.7) | data formatting | bytes 851968
  141.2 1.8 %copy.12 = bf16[128,1664]{1,0:T(8,128)(2,1)} copy(bf16[128,1664]{1,0:T(8,128)(2,1)} %get-tuple-element.8) | data formatting | bytes 851968

commit v3 on v1

v3 whole, which is shorter than its diff:
```python
import jax
import jax.numpy as jnp
from jax import lax
from jax.experimental import pallas as pl
from jax.experimental.pallas import tpu as pltpu
from jax.sharding import PartitionSpec as P

BF16, F32 = jnp.bfloat16, jnp.float32

Z_THEN_Y = 1408
Y_THEN_Z = 1280

ORDER = [
    "gz", "h0.sA", "g0.spread", "h0.sB", "qy.spread", "hz.spread", "g1.spread", "g0.sp", "h0.rp", "h0.rm",
    "qy.rp", "qy.rm", "g1.rm", "g0.sm", "g1.rp", "g1.sm", "h1.sA", "h2.sB", "g1.sf", "hz.rm", "g0.rp",
    "hz.rp", "g0.rm", "qz.spread", "h2.sA", "h2.rm", "g0.sf", "g1.sp", "h1.sB", "h2.rp", "bwd3", "h1.rp",
    "fwd0", "h3.sA", "bwd0", "qz.rm", "qz.rp", "h1.rm", "bwd1", "h3.sB", "rz.far", "op0", "p1.far", "bwd2",
    "p3.far", "fwdP", "fwdO", "rz.nearm", "rz.nearp", "h3.rm", "h3.rp", "p3.near", "opO", "p3.rp", "p3.rm",
    "opP", "o0.start", "fwd3", "rz.rm", "rz.rp", "o0.rm", "p1.rp", "p2.far", "p1.rm", "o0.rp", "op3",
    "o1.start", "p3.here", "pz.far", "p1.near", "p2.rm", "o0.here", "o1.rp", "p2.near", "p2.rp", "p0.far",
    "o1.rm", "o1.here", "oz", "p1.here", "ry.start", "pz.rm", "p2.here", "pz.nearp", "pz.rp", "p0.near",
    "ry.rm", "p0.rm", "p0.rp", "oend", "ry.rp", "pz.nearm", "fin",
]
SEMAPHORES = 128


def kernel(
    gate, up, weight_hbm, cot, out, gate_grad, up_grad,
    weight, hid, cots, part_out, part_grad,
    from_sib, x_full, x_half, x_sum, zl_in,
    y_full, y_half, y_sum, z_full, z_half,
    qz_full, qz_half, q_sum, qy_full, qy_half,
    send_sems, recv_sems, load_sems,
):
    tokens, units = gate.shape
    feats = weight.shape[1]
    half = tokens // 2
    A, B, ALL = pl.ds(0, half), pl.ds(half, half), pl.ds(0, tokens)
    H_FIRST, H_REST = pl.ds(0, Z_THEN_Y), pl.ds(Z_THEN_Y, units - Z_THEN_Y)
    G_FIRST, G_REST = pl.ds(0, Y_THEN_Z), pl.ds(Y_THEN_Z, units - Y_THEN_Z)

    row, col = lax.axis_index("row"), lax.axis_index("col")
    zl, x, core = row // 8, (row // 2) % 4, row % 2
    z, y = col // 4, col % 4
    xs = {d: (x + d) % 4 for d in (0, 1, 2, 3)}
    ys = {d: (y + d) % 4 for d in (0, 1, 2, 3)}
    zs = {d: (z + d) % 4 for d in (0, 1, 2, 3)}

    def at_row(zl_, x_, core_):
        return zl_ * 8 + x_ * 2 + core_

    def at_col(z_, y_):
        return z_ * 4 + y_

    near = {
        "xp": {"row": at_row(zl, xs[1], core)},
        "xm": {"row": at_row(zl, xs[3], core)},
        "zl": {"row": at_row(1 - zl, x, core)},
        "sib": {"row": at_row(zl, x, 1 - core)},
        "yp": {"col": at_col(z, ys[1])},
        "ym": {"col": at_col(z, ys[3])},
        "zp": {"col": at_col(zs[1], y)},
        "zm": {"col": at_col(zs[3], y)},
    }

    numbers, awaited, sent, lands, tasks = {}, set(), [], {}, {}

    def copy(name, src, dst, to):
        number = numbers.setdefault(name, len(numbers))
        return pltpu.make_async_remote_copy(
            src_ref=src,
            dst_ref=dst,
            send_sem=send_sems.at[number],
            recv_sem=recv_sems.at[number],
            device_id=near[to],
            device_id_type=pl.DeviceIdType.MESH,
        )

    def send(name, src, dst, to):
        one = copy(name, src, dst, to)
        one.start()
        sent.append(one)

    def wait(*names):
        for name in names:
            if name not in awaited:
                awaited.add(name)
                copy(name, lands[name], lands[name], "sib").wait_recv()

    def chunks(count, body):
        def step(i, carry):
            body(pl.ds(pl.multiple_of(i * 16, 16), 16))
            return carry

        lax.fori_loop(0, count // 16, step, 0)

    def sum_to(ref, terms):
        lead = (slice(None),) * (len(ref.shape) - 2)

        def body(rows):
            index = lead + (rows,)
            total = terms[0][index].astype(F32)
            for term in terms[1:]:
                total = total + term[index].astype(F32)
            ref[index] = total.astype(BF16)

        chunks(ref.shape[-2], body)

    class Gather:
        def __init__(self, name, axis, block):
            self.name, self.plus, self.minus, self.block = name, axis + "p", axis + "m", block
            lands.update({
                name + "pA": block(3, A), name + "pB": block(3, B), name + "hp": block(2, A),
                name + "mA": block(1, A), name + "mB": block(1, B), name + "hm": block(2, B),
            })
            tasks[name + ".rp"] = self.relay_plus
            tasks[name + ".rm"] = self.relay_minus

        def push(self, what, d, part, to):
            send(self.name + what, self.block(d, part), self.block(d, part), to)

        def spread_a(self):
            self.push("pA", 0, A, self.plus)
            self.push("mA", 0, A, self.minus)

        def spread_b(self):
            self.push("mB", 0, B, self.minus)
            self.push("pB", 0, B, self.plus)

        def spread(self):
            self.push("pA", 0, A, self.plus)
            self.push("mB", 0, B, self.minus)
            self.push("pB", 0, B, self.plus)
            self.push("mA", 0, A, self.minus)

        def relay_plus(self):
            wait(self.name + "pA")
            self.push("hp", 3, A, self.plus)

        def relay_minus(self):
            wait(self.name + "mB")
            self.push("hm", 1, B, self.minus)

        def wait_all(self):
            wait(*[self.name + what for what in ("pA", "pB", "mA", "mB", "hp", "hm")])

    class Scatter:
        def __init__(self, name, axis, part, full, halves):
            self.name, self.plus, self.minus, self.part = name, axis + "p", axis + "m", part
            self.full, self.halves = full, halves
            lead = (slice(None),) * (len(full.shape) - 3)
            self.slot = lambda side, rows: full.at[(side,) + lead + (rows,)]
            lands.update({
                name + "pA": self.slot(0, A), name + "pB": self.slot(0, B), name + "hp": halves.at[0],
                name + "mA": self.slot(1, A), name + "mB": self.slot(1, B), name + "hm": halves.at[1],
            })
            tasks[name + ".far"] = self.far
            tasks[name + ".near"] = self.near
            tasks[name + ".nearp"] = self.near_plus
            tasks[name + ".nearm"] = self.near_minus
            tasks[name + ".rp"] = self.relay_plus
            tasks[name + ".rm"] = self.relay_minus

        def far(self):
            send(self.name + "hp", self.part(2, A), self.halves.at[0], self.plus)
            send(self.name + "hm", self.part(2, B), self.halves.at[1], self.minus)

        def near_plus(self):
            send(self.name + "pB", self.part(1, B), self.slot(0, B), self.plus)

        def near_minus(self):
            send(self.name + "mA", self.part(3, A), self.slot(1, A), self.minus)

        def near(self):
            self.near_plus()
            self.near_minus()

        def relay_plus(self):
            wait(self.name + "hp")
            sum_to(self.part(1, A), (self.part(1, A), self.halves.at[0]))
            send(self.name + "pA", self.part(1, A), self.slot(0, A), self.plus)

        def relay_minus(self):
            wait(self.name + "hm")
            sum_to(self.part(3, B), (self.part(3, B), self.halves.at[1]))
            send(self.name + "mB", self.part(3, B), self.slot(1, B), self.minus)

        def wait_all(self):
            wait(*[self.name + what for what in ("pA", "pB", "mA", "mB")])

    def task(function):
        tasks[function.__name__.replace("_", ".")] = function

    zls = (zl, 1 - zl)
    g = []
    for k in range(2):

        def g_block(d, rows=ALL, core_=core, zl_=zls[k]):
            return cots.at[at_row(zl_, xs[d], core_), rows]

        ring = Gather(f"g{k}", "x", g_block)
        g.append(ring)
        for what, d in (("s", 0), ("sm", 3), ("sp", 1), ("sf", 2)):
            lands[f"g{what}{k}"] = g_block(d, core_=1 - core)

        def g_spread(k=k, ring=ring):
            if k:
                wait("gz")
            ring.spread()
            send(f"gs{k}", ring.block(0), ring.block(0), "sib")

        def g_sib(what, d, needs, k=k, ring=ring):
            wait(*[f"g{k}{need}" for need in needs])
            send(f"g{what}{k}", ring.block(d), ring.block(d), "sib")

        tasks[f"g{k}.spread"] = g_spread
        tasks[f"g{k}.sm"] = lambda f=g_sib: f("sm", 3, ("pA", "pB"))
        tasks[f"g{k}.sp"] = lambda f=g_sib: f("sp", 1, ("mA", "mB"))
        tasks[f"g{k}.sf"] = lambda f=g_sib: f("sf", 2, ("hp", "hm"))
    lands["gz"] = g[1].block(0)

    @task
    def gz():
        send("gz", g[0].block(0), g[0].block(0), "zl")

    def wait_cots():
        wait("gz")
        for k in range(2):
            g[k].wait_all()
            wait(*[f"g{what}{k}" for what in ("s", "sm", "sp", "sf")])
        if "weight" not in awaited:
            awaited.add("weight")
            load_weight.wait()

    hz = Gather("hz", "z", lambda d, rows: hid.at[at_col(zs[d], y), rows, H_FIRST])
    qy = Gather("qy", "y", lambda d, rows: hid.at[at_col(z, ys[d]), rows, H_REST])
    qz = Gather("qz", "z", lambda d, rows: hid.at[pl.ds(zs[d] * 4, 4), rows, H_REST])
    set_z = (zs[0], zs[3], zs[1], zs[2])
    h = [
        Gather(f"h{k}", "y", lambda d, rows, z_=set_z[k]: hid.at[at_col(z_, ys[d]), rows, H_FIRST]) for k in range(4)
    ]
    tasks["hz.spread"] = hz.spread
    tasks["qy.spread"] = qy.spread

    @task
    def qz_spread():
        qy.wait_all()
        qz.spread()

    for k, needs in enumerate((None, ("hzpA", "hzpB"), ("hzmA", "hzmB"), ("hzhp", "hzhm"))):

        def h_first(k=k, needs=needs):
            if needs:
                wait(needs[0])
            h[k].spread_a()

        def h_second(k=k, needs=needs):
            if needs:
                wait(needs[1])
            h[k].spread_b()

        tasks[f"h{k}.sA"], tasks[f"h{k}.sB"] = h_first, h_second

    p = [
        Scatter(
            f"p{k}", "y",
            lambda d, rows, z_=set_z[k]: part_grad.at[at_col(z_, ys[d]), rows, G_FIRST],
            y_full.at[k], y_half.at[k],
        )
        for k in range(4)
    ]
    pz = Scatter("pz", "z", lambda d, rows: y_sum.at[{3: 0, 1: 1, 2: 2}[d], rows], z_full, z_half)
    rz = Scatter("rz", "z", lambda d, rows: part_grad.at[pl.ds(zs[d] * 4, 4), rows, G_REST], qz_full, qz_half)
    ry = Scatter("ry", "y", lambda d, rows: q_sum.at[ys[d], rows], qy_full, qy_half)

    def backward(z_):
        wait_cots()
        four = pl.ds(z_ * 4, 4)

        def tile(start, width):
            left = cots[four].reshape(4 * tokens, feats)
            product = lax.dot_general(
                left, weight[pl.ds(start, width)], (((1,), (1,)), ((), ())), preferred_element_type=F32
            )
            part_grad[four, :, pl.ds(start, width)] = product.astype(BF16).reshape(4, tokens, width)

        def step(i, carry):
            tile(pl.multiple_of(i * 256, 256), 256)
            return carry

        lax.fori_loop(0, units // 256, step, 0)
        if units % 256:
            tile(units // 256 * 256, units % 256)

    for k in range(4):
        tasks[f"bwd{k}"] = lambda k=k: backward(set_z[k])

    def p_here(k):
        p[k].wait_all()
        sum_to(y_sum.at[k - 1], (p[k].part(0, ALL), y_full.at[k, 0], y_full.at[k, 1]))

    for k in range(1, 4):
        tasks[f"p{k}.here"] = lambda k=k: p_here(k)

    @task
    def ry_start():
        rz.wait_all()
        sum_to(q_sum, (rz.part(0, ALL), qz_full.at[0], qz_full.at[1]))
        ry.far()
        ry.near()

    def forward(name, z_):
        four, chips = pl.ds(z_ * 4, 4), pl.ds(z_ * 2, 2)

        def step(i, carry):
            columns = pl.ds(pl.multiple_of(i * 256, 256), 256)
            left = hid[four].reshape(4 * tokens, units)
            product = jnp.dot(left, weight[:, columns], preferred_element_type=F32).astype(BF16)
            for j in range(4):
                part_out[j % 2, z_ * 2 + j // 2, :, columns] = product[j * tokens : (j + 1) * tokens]
            return carry

        lax.fori_loop(0, feats // 256, step, 0)
        lands["od" + name] = from_sib.at[chips]
        send("od" + name, part_out.at[1 - core, chips], from_sib.at[chips], "sib")

    def add_sibling(name, z_):
        chips = pl.ds(z_ * 2, 2)
        wait("od" + name)
        sum_to(part_out.at[core, chips], (part_out.at[core, chips], from_sib.at[chips]))

    pair = z + 1 - 2 * (z % 2)
    other = zs[1] + zs[3] - pair

    @task
    def fwd0():
        qy.wait_all()
        h[0].wait_all()
        forward("0", z)

    def wait_middle():
        wait("hzpA", "hzpB", "hzmA", "hzmB", "qzpA", "qzpB", "qzmA", "qzmB")
        h[1].wait_all()
        h[2].wait_all()

    @task
    def fwdP():
        wait_middle()
        forward("P", pair)

    @task
    def fwdO():
        wait_middle()
        forward("O", other)

    @task
    def fwd3():
        hz.wait_all()
        qz.wait_all()
        h[3].wait_all()
        forward("3", zs[2])

    for name, z_ in (("0", z), ("P", pair), ("O", other), ("3", zs[2])):
        tasks["op" + name] = lambda name=name, z_=z_: add_sibling(name, z_)

    o_zl = (z // 2, 1 - z // 2)
    o = [
        Scatter(
            f"o{m}", "x", lambda d, rows, zl_=o_zl[m]: part_out.at[core, zl_ * 4 + xs[d], rows], x_full.at[m], x_half.at[m]
        )
        for m in range(2)
    ]

    def o_start(m):
        o[m].far()
        o[m].near()

    def o_here(m):
        o[m].wait_all()
        sum_to(x_sum.at[o_zl[m]], (o[m].part(0, ALL), x_full.at[m, 0], x_full.at[m, 1]))

    for m in range(2):
        tasks[f"o{m}.start"] = lambda m=m: o_start(m)
        tasks[f"o{m}.here"] = lambda m=m: o_here(m)
    lands["oz"] = zl_in

    @task
    def oz():
        send("oz", x_sum.at[1 - zl], zl_in, "zl")

    @task
    def oend():
        wait("oz")
        sum_to(out, (x_sum.at[zl], zl_in))

    def finish(rows, columns, terms):
        grad = terms[0].astype(F32)
        for term in terms[1:]:
            grad = grad + term.astype(F32)
        gate_value = gate[rows, columns].astype(F32)
        up_value = up[rows, columns].astype(F32)
        sigma = 1.0 / (1.0 + jnp.exp(-gate_value))
        scaled = grad * sigma
        gate_grad[rows, columns] = (scaled * up_value * (1.0 + gate_value * (1.0 - sigma))).astype(BF16)
        up_grad[rows, columns] = (scaled * gate_value).astype(BF16)

    @task
    def fin():
        p[0].wait_all()
        pz.wait_all()
        ry.wait_all()

        def last(rows):
            here = part_grad[col, rows, G_FIRST]
            finish(rows, G_FIRST, (here, y_full[0, 0, rows], y_full[0, 1, rows], z_full[0, rows], z_full[1, rows]))
            finish(rows, G_REST, (q_sum[y, rows], qy_full[0, rows], qy_full[1, rows]))

        chunks(tokens, last)

    barrier = pltpu.get_barrier_semaphore()
    for to in near.values():
        pl.semaphore_signal(barrier, inc=1, device_id=to, device_id_type=pl.DeviceIdType.MESH)
    load_cot = pltpu.make_async_copy(cot, cots.at[row], load_sems.at[0])
    load_cot.start()
    load_weight = pltpu.make_async_copy(weight_hbm, weight, load_sems.at[1])
    load_weight.start()

    def make_hidden(rows):
        value = gate[rows].astype(F32)
        silu = value / (1.0 + jnp.exp(-value))
        hid[col, rows] = (silu * up[rows].astype(F32)).astype(BF16)

    chunks(tokens, make_hidden)
    load_cot.wait()
    pl.semaphore_wait(barrier, len(near))

    for name in ORDER:
        tasks[name]()
    for one in sent:
        one.wait_send()


def local(gate_pre, up_pre, down_weight, out_grad):
    tokens, units = gate_pre.shape
    feats = out_grad.shape[1]
    half = tokens // 2
    first, rest = Y_THEN_Z, units - Y_THEN_Z

    def vmem(*shape):
        return pltpu.VMEM(shape, BF16)

    whole = pl.BlockSpec(memory_space=pltpu.VMEM)
    outside = pl.BlockSpec(memory_space=pl.ANY)
    return pl.pallas_call(
        kernel,
        out_shape=(
            jax.ShapeDtypeStruct((tokens, feats), BF16),
            jax.ShapeDtypeStruct((tokens, units), BF16),
            jax.ShapeDtypeStruct((tokens, units), BF16),
        ),
        in_specs=[whole, whole, outside, outside],
        out_specs=(whole,) * 3,
        scratch_shapes=[
            vmem(units, feats),
            vmem(16, tokens, units),
            vmem(16, tokens, feats),
            vmem(2, 8, tokens, feats),
            vmem(16, tokens, units),
            vmem(8, tokens, feats),
            vmem(2, 2, tokens, feats),
            vmem(2, 2, half, feats),
            vmem(2, tokens, feats),
            vmem(tokens, feats),
            vmem(4, 2, tokens, first),
            vmem(4, 2, half, first),
            vmem(3, tokens, first),
            vmem(2, tokens, first),
            vmem(2, half, first),
            vmem(2, 4, tokens, rest),
            vmem(2, 4, half, rest),
            vmem(4, tokens, rest),
            vmem(2, tokens, rest),
            vmem(2, half, rest),
            pltpu.SemaphoreType.DMA((SEMAPHORES,)),
            pltpu.SemaphoreType.DMA((SEMAPHORES,)),
            pltpu.SemaphoreType.DMA((2,)),
        ],
        compiler_params=pltpu.CompilerParams(
            collective_id=0, has_side_effects=True, vmem_limit_bytes=60 * 1024 * 1024
        ),
        cost_estimate=pl.CostEstimate(
            flops=4 * 16 * tokens * units * feats, bytes_accessed=8 * 1024 * 1024, transcendentals=0
        ),
    )(gate_pre, up_pre, down_weight, out_grad)


def solution(mesh):
    return jax.shard_map(
        local,
        mesh=mesh,
        in_specs=(P("col", "row"), P("col", "row"), P("row", "col"), P("row", "col")),
        out_specs=(P("row", "col"), P("col", "row"), P("col", "row")),
        check_vma=False,
    )
```

time: 368 us -> 128 us (0.35)
  waiting for transfers between devices: 325 us -> 0 us
  Pallas kernels: 0 us -> 121 us
  matrix products: 22.6 us -> 0 us
  between operations: 13.8 us -> 0.64 us
  local copies, waits for them, and re-layouts: 0.01 us -> 5.26 us
    reduce_scatter x2 -> x0, waiting for transfers between devices: 185 us -> none  [the longest x1 112 us: local(): lax.psum_scatter(partial_grad.astype(jnp.bfloat16), 'col', scatter_dimens...]
    all_gather x2 -> x0, waiting for transfers between devices: 140 us -> none  [the longest x1 94 us: local(): lax.all_gather(hidden_of(gate_pre, up_pre), 'col', axis=0, tiled=True)]
    pallas_call x0 -> x1, Pallas kernels: none -> 121 us  [local(): pl.pallas_call(kernel, out_shape=(jax.ShapeDtypeStruct((tokens, feats), B...]
    dot_general x2 -> x0, matrix products: 22.6 us -> none  [the longest x1 11.4 us: local(): lax.dot_general(lax.all_gather(out_grad, 'row', axis=0, tiled=True), down...]
    unnamed x2 -> x3, local copies, waits for them, and re-layouts: 0.01 us -> 5.26 us
  transfers between devices with their start and end apart: 4 -> 0, of which waited for: 4 -> 0; matrix products, arithmetic and copies ran while one was open for 0% -> 0% of each run, Pallas kernels for 0% -> 0%
where the time goes in v3:
time: 128 us; the launch traced here: 127 us
  Pallas kernels  121 us (95%)
  local copies, waits for them, and re-layouts  5.26 us (4%)
    pallas_call x1, Pallas kernels, local(): pl.pallas_call(kernel, out_shape=(jax.ShapeDtypeStruct((tokens, feats), B...  121 us
    unnamed x3, local copies, waits for them, and re-layouts  5.26 us

profile of v3, /device:TPU:1, one launch (start us, length us, event | category | flops | bytes accessed | tf_op | source)
XLA Modules:
  0.0 126.9 jit_solution(18216345149559062434)
XLA Ops:
  0.6 121.0 %shard_map.67 = (bf16[128,1024]{1,0:T(8,128)(2,1)}, bf16[128,1664]{1,0:T(8,128)(2,1)}, bf16[128,1664]{1,0:T(8,128)(2,1)}) custom-call(bf16[128,1664]{1,0:T(8,128)(2,1)} %gate.1, bf16[128,1664]{1,0:T(8,128)(2,1)} %up.1, bf16[1664,1024]{1,0:T(8,128)(2,1)} %weight_hbm.1, bf16[128,1024]{1,0:T(8,128)(2,1)} %cot.1), custom_call_target="tpu_custom_call" | custom-call | flops 13958643712 | bytes 8388608 | tf_op jit(solution)/shard_map/pallas_call | solution.py:454
  121.7 1.7 %copy.10 = bf16[128,1024]{1,0:T(8,128)(2,1)} copy(bf16[128,1024]{1,0:T(8,128)(2,1)} %get-tuple-element.6) | data formatting | bytes 524288
  123.4 1.8 %copy.11 = bf16[128,1664]{1,0:T(8,128)(2,1)} copy(bf16[128,1664]{1,0:T(8,128)(2,1)} %get-tuple-element.7) | data formatting | bytes 851968
  125.1 1.8 %copy.12 = bf16[128,1664]{1,0:T(8,128)(2,1)} copy(bf16[128,1664]{1,0:T(8,128)(2,1)} %get-tuple-element.8) | data formatting | bytes 851968

commit v4 on v1

v4 whole, which is shorter than its diff:
```python
import jax
import jax.numpy as jnp
from jax import lax
from jax.experimental import pallas as pl
from jax.experimental.pallas import tpu as pltpu
from jax.sharding import PartitionSpec as P

BF16, F32 = jnp.bfloat16, jnp.float32

CHUNKS = 4
Z_FIRST = (0,)

ORDER = [
    10, 12, 18, 0, 1, 39, 14, 41, 13, 24, 16, 11,
    42, 40, 5, 101, 30, 15, 45, 102, 36, 25, 43,
    37, 9, 3, 32, 99, 44, 22, 17, 20, 100, 26, 7,
    103, 46, 38, 104, 19, 27, 115, 31, 107, 28,
    116, 2, 21, 8, 108, 105, 106, 117, 34, 6, 47,
    111, 109, 23, 35, 33, 164, 29, 162, 118, 128,
    110, 48, 119, 58, 50, 112, 165, 166, 57, 51,
    113, 163, 175, 56, 127, 4, 52, 126, 97, 96,
    114, 168, 173, 167, 174, 121, 53, 54, 169,
    183, 84, 95, 82, 120, 88, 122, 135, 89, 87,
    139, 137, 182, 90, 75, 76, 181, 141, 71, 143,
    86, 91, 140, 138, 150, 83, 73, 93, 70, 92,
    144, 129, 62, 142, 158, 63, 69, 184, 185, 78,
    149, 176, 148, 177, 74, 79, 77, 55, 49, 156,
    80, 94, 157, 133, 68, 134, 61, 60, 66, 151,
    152, 67, 159, 160, 64, 65, 81, 98, 59, 136,
    186, 72, 161, 85, 188, 187,
]
SEMAPHORES = 256


def kernel(
    gate_hbm, up_hbm, weight_hbm, cot, out, grad,
    gate, up, weight, weight_in, hid_own, hid, hid_set, cots, part_out, from_sib,
    x_full, x_half, x_sum, pair_in, zl_in,
    part_grad, q_in, z_full, z_half, zq_full, zq_half, fy_out, fy_in, grad_t,
    send_sems, recv_sems, load_sems,
):
    tokens, units = gate.shape
    feats = weight.shape[1]
    half, mine = tokens // 2, units // 2
    step_rows = mine // CHUNKS
    A, B, ALL = pl.ds(0, half), pl.ds(half, half), pl.ds(0, tokens)

    row, col = lax.axis_index("row"), lax.axis_index("col")
    zl, x, core = row // 8, (row // 2) % 4, row % 2
    z, y = col // 4, col % 4
    y_pair, y_q = y + 1 - 2 * (y % 2), 3 - y
    kind = (y % 2 + y // 2) % 2
    here, there = y // 2 * 2, 2 - y // 2 * 2
    xs = {d: (x + d) % 4 for d in (0, 1, 2, 3)}
    zs = {d: (z + d) % 4 for d in (0, 1, 2, 3)}

    def at_row(zl_, x_, core_):
        return zl_ * 8 + x_ * 2 + core_

    def at_col(z_, y_):
        return z_ * 4 + y_

    near = {
        "xp": {"row": at_row(zl, xs[1], core)},
        "xm": {"row": at_row(zl, xs[3], core)},
        "zl": {"row": at_row(1 - zl, x, core)},
        "sib": {"row": at_row(zl, x, 1 - core)},
        "pr": {"col": at_col(z, y_pair)},
        "q": {"col": at_col(z, y_q)},
        "zp": {"col": at_col(zs[1], y)},
        "zm": {"col": at_col(zs[3], y)},
    }

    numbers, awaited, sent, lands, tasks = {}, set(), [], {}, {}

    def copy(name, src, dst, to):
        number = numbers.setdefault(name, len(numbers))
        return pltpu.make_async_remote_copy(
            src_ref=src,
            dst_ref=dst,
            send_sem=send_sems.at[number],
            recv_sem=recv_sems.at[number],
            device_id=near[to],
            device_id_type=pl.DeviceIdType.MESH,
        )

    def send(name, src, dst, to):
        one = copy(name, src, dst, to)
        one.start()
        sent.append(one)

    def wait(*names):
        for name in names:
            if name not in awaited:
                awaited.add(name)
                copy(name, lands[name], lands[name], "sib").wait_recv()

    def chunks(count, body):
        def step(i, carry):
            body(pl.ds(pl.multiple_of(i * 16, 16), 16))
            return carry

        lax.fori_loop(0, count // 16, step, 0)

    def sum_to(ref, terms):
        lead = (slice(None),) * (len(ref.shape) - 2)

        def body(rows):
            index = lead + (rows,)
            ref[index] = total_of([term[index] for term in terms]).astype(BF16)

        count, columns = ref.shape[-2:]
        if columns > 128:
            chunks(count, body)
        else:
            for start in range(0, count, 16):
                body(pl.ds(start, 16))

    def total_of(terms):
        result = terms[0].astype(F32)
        for term in terms[1:]:
            result = result + term.astype(F32)
        return result

    class Gather:
        def __init__(self, name, axis, block):
            self.name, self.plus, self.minus, self.block = name, axis + "p", axis + "m", block
            lands.update({
                name + "pA": block(3, A), name + "pB": block(3, B), name + "hp": block(2, A),
                name + "mA": block(1, A), name + "mB": block(1, B), name + "hm": block(2, B),
            })
            tasks[name + ".rp"] = self.relay_plus
            tasks[name + ".rm"] = self.relay_minus

        def push(self, what, d, part, to):
            send(self.name + what, self.block(d, part), self.block(d, part), to)

        def spread_a(self):
            self.push("pA", 0, A, self.plus)
            self.push("mA", 0, A, self.minus)

        def spread_b(self):
            self.push("mB", 0, B, self.minus)
            self.push("pB", 0, B, self.plus)

        def spread(self):
            self.push("pA", 0, A, self.plus)
            self.push("mB", 0, B, self.minus)
            self.push("pB", 0, B, self.plus)
            self.push("mA", 0, A, self.minus)

        def relay_plus(self):
            wait(self.name + "pA")
            self.push("hp", 3, A, self.plus)

        def relay_minus(self):
            wait(self.name + "mB")
            self.push("hm", 1, B, self.minus)

        def wait_all(self):
            wait(*[self.name + what for what in ("pA", "pB", "mA", "mB", "hp", "hm")])

    class Scatter:
        def __init__(self, name, axis, part, slot, halves):
            self.name, self.plus, self.minus, self.part = name, axis + "p", axis + "m", part
            self.slot, self.halves = slot, halves
            lands.update({
                name + "pA": self.slot(0, A), name + "pB": self.slot(0, B), name + "hp": halves(0),
                name + "mA": self.slot(1, A), name + "mB": self.slot(1, B), name + "hm": halves(1),
            })
            tasks[name + ".far"] = self.far
            tasks[name + ".nearp"] = self.near_plus
            tasks[name + ".nearm"] = self.near_minus
            tasks[name + ".rp"] = self.relay_plus
            tasks[name + ".rm"] = self.relay_minus

        def far(self):
            send(self.name + "hp", self.part(2, A), self.halves(0), self.plus)
            send(self.name + "hm", self.part(2, B), self.halves(1), self.minus)

        def near_plus(self):
            send(self.name + "pB", self.part(1, B), self.slot(0, B), self.plus)

        def near_minus(self):
            send(self.name + "mA", self.part(3, A), self.slot(1, A), self.minus)

        def near(self):
            self.near_plus()
            self.near_minus()

        def relay_plus(self):
            wait(self.name + "hp")
            sum_to(self.part(1, A), (self.part(1, A), self.halves(0)))
            send(self.name + "pA", self.part(1, A), self.slot(0, A), self.plus)

        def relay_minus(self):
            wait(self.name + "hm")
            sum_to(self.part(3, B), (self.part(3, B), self.halves(1)))
            send(self.name + "mB", self.part(3, B), self.slot(1, B), self.minus)

        def wait_all(self):
            wait(*[self.name + what for what in ("pA", "pB", "mA", "mB")])

    def task(function):
        tasks[function.__name__.replace("_", ".")] = function

    @task
    def hid_():
        load_gate.wait()
        load_up.wait()
        for u in range(0, units, 128):
            columns = pl.ds(u, 128)
            value = gate[:, columns].astype(F32)
            silu = value / (1.0 + jnp.exp(-value))
            hidden = silu * up[:, columns].astype(F32)
            hid_own[columns] = hidden.T.astype(BF16)
        hid[col] = hid_own[pl.ds(pl.multiple_of(kind * mine, 16), mine)]

    @task
    def e0():
        rows = pl.ds(pl.multiple_of((1 - kind) * mine, 16), mine)
        send("e0", hid_own.at[rows], hid.at[col], "pr")

    lands["e0"] = hid.at[at_col(z, y_pair)]

    def chunk(j):
        return pl.ds(j * step_rows, step_rows)

    columns_of = {"0": pl.ds(0, feats), "a": pl.ds(0, feats // 2), "b": pl.ds(feats // 2, feats // 2)}

    def w_send(j, e):
        if "weight" not in awaited:
            awaited.add("weight")
            load_weight.wait()
        rows = pl.ds(pl.multiple_of((1 - kind) * mine + j * step_rows, 16), step_rows)
        send(f"w{j}{e}", weight.at[rows, columns_of[e]], weight_in.at[chunk(j), columns_of[e]], "pr")

    for j in range(CHUNKS):
        for e in "ab":
            lands[f"w{j}{e}"] = weight_in.at[chunk(j), columns_of[e]]
            tasks[f"w{j}{e}"] = lambda j=j, e=e: w_send(j, e)

    @task
    def c1():
        send("c1", cots.at[0, row], cots.at[1, row], "pr")

    @task
    def c2():
        wait("gz")
        away = at_row(1 - zl, x, core)
        send("c2", cots.at[0, away], cots.at[1, away], "pr")

    lands["c1"] = cots.at[1, row]
    lands["c2"] = cots.at[1, at_row(1 - zl, x, core)]
    zls = (zl, 1 - zl)
    g = {}

    def g_spread(name, ring, needs):
        wait(*needs)
        ring.spread()
        send(name + "s", ring.block(0), ring.block(0), "sib")

    def g_sib(name, ring, what, d, needs):
        wait(*[name + need for need in needs])
        send(name + what, ring.block(d), ring.block(d), "sib")

    @task
    def gz():
        send("gz", cots.at[0, row], cots.at[0, row], "zl")

    lands["gz"] = cots.at[0, at_row(1 - zl, x, core)]

    for i in range(2):
        for k in range(2):

            def g_block(d, rows=ALL, core_=core, i=i, zl_=zls[k]):
                return cots.at[i, at_row(zl_, xs[d], core_), rows]

            name = f"g{i}{k}"
            ring = g[i, k] = Gather(name, "x", g_block)
            for what, d, needs in (
                ("s", 0, ()), ("sm", 3, ("pA", "pB")), ("sp", 1, ("mA", "mB")), ("sf", 2, ("hp", "hm"))
            ):
                lands[name + what] = g_block(d, core_=1 - core)
                if needs:
                    tasks[f"{name}.{what}"] = lambda *a, args=(name, ring, what, d, needs): g_sib(*args)
            needs = ("gz", "c2")[i : i + 1] if k else ("c1",) if i else ()
            tasks[name + ".spread"] = lambda args=(name, ring, needs): g_spread(*args)

    def wait_cots():
        for i in range(2):
            for k in range(2):
                g[i, k].wait_all()
                wait(*[f"g{i}{k}{what}" for what in ("s", "sm", "sp", "sf")])

    def hid_block(z_, part):
        return hid.at[at_col(z_, y if part is A else y_pair)]

    hz = Gather("hz", "z", lambda d, part: hid_block(zs[d], part))
    pair = z + 1 - 2 * (z % 2)
    other = zs[1] + zs[3] - pair
    hid_z = (zs[0], pair, other, zs[2])
    set_z = (zs[0], zs[3], zs[1], zs[2])

    def hz_first():
        hz.spread_a()

    def hz_second():
        wait("e0")
        hz.spread_b()

    tasks["hz.sA"], tasks["hz.sB"] = hz_first, hz_second

    def h_send(k, part, needs):
        wait(*needs)
        block = hid_block(hid_z[k], part)
        send(f"h{k}" + ("A" if part is A else "B"), block, block, "q")

    first_near, second_near = ("hzpA", "hzmA"), ("hzpB", "hzmB")
    arrivals = (((), ("e0",)), (first_near, second_near), (first_near, second_near), (("hzhp",), ("hzhm",)))
    for k, (first, second) in enumerate(arrivals):
        lands[f"h{k}A"] = hid.at[at_col(hid_z[k], y_q)]
        lands[f"h{k}B"] = hid.at[at_col(hid_z[k], 3 - y_pair)]
        tasks[f"h{k}.A"] = lambda k=k, needs=first: h_send(k, A, needs)
        tasks[f"h{k}.B"] = lambda k=k, needs=second: h_send(k, B, needs)

    def q_send(k, j):
        send(f"s{k}{j}", part_grad.at[pl.ds(set_z[k] * 4 + there, 2), chunk(j)], q_in.at[k, :, chunk(j)], "q")

    def backward(k, j):
        wait_cots()
        wait(f"w{j}a", f"w{j}b")
        if "weight" not in awaited:
            awaited.add("weight")
            load_weight.wait()
        four = pl.ds(set_z[k] * 4, 4)
        own = pl.ds(pl.multiple_of(kind * mine + j * step_rows, 16), step_rows)
        total = None
        for i, rows in enumerate((weight[own], weight_in[chunk(j)])):
            right = cots[i, four].reshape(4 * tokens, feats)
            product = lax.dot_general(rows, right, (((1,), (1,)), ((), ())), preferred_element_type=F32)
            total = product if total is None else total + product
        total = total.astype(BF16)
        for b in range(4):
            part_grad[set_z[k] * 4 + b, chunk(j)] = total[:, b * tokens : (b + 1) * tokens]
        if j not in Z_FIRST:
            q_send(k, j)

    def q_add(k, j):
        wait(f"s{k}{j}")
        two = part_grad.at[pl.ds(set_z[k] * 4 + here, 2), chunk(j)]
        sum_to(two, (two, q_in.at[k, :, chunk(j)]))

    def pair_end(j):
        wait(f"s0{j}")
        p_rings[j].wait_all()
        sides = () if j in Z_FIRST else (0, 1)
        own, others = at_col(z, y), at_col(z, y_pair)
        to = pl.multiple_of(kind * mine + j * step_rows, 16)

        for i in range(step_rows // 16):
            rows = pl.ds(j * step_rows + i * 16, 16)
            fy_out[rows] = total_of(
                [part_grad[others, rows], q_in[0, 1 - y % 2, rows]] + [z_full[side, 1, rows] for side in sides]
            ).astype(BF16)
            grad_t[pl.ds(to + i * 16, 16)] = total_of(
                [part_grad[own, rows], q_in[0, y % 2, rows]] + [z_full[side, 0, rows] for side in sides]
            )
        send(f"fy{j}", fy_out.at[chunk(j)], fy_in.at[chunk(j)], "pr")

    def z_first_end(j):
        p_rings[j].wait_all()
        for start, part in ((there, 2), (here, 0)):
            two = part_grad.at[pl.ds(z * 4 + start, 2), chunk(j)]
            sum_to(two, (two, zq_full.at[0, part : part + 2], zq_full.at[1, part : part + 2]))
            if part:
                q_send(0, j)

    p_rings = []
    for j in range(CHUNKS):
        if j in Z_FIRST:

            def part(d, which, j=j):
                return part_grad.at[pl.ds(zs[d] * 4 + (here if which is A else there), 2), chunk(j)]

            def slot(side, which):
                return zq_full.at[side, 0:2] if which is A else zq_full.at[side, 2:4]

            def halves(side):
                return zq_half.at[side]

            tasks[f"sq{j}"] = lambda j=j: z_first_end(j)
        else:

            def part(d, which, j=j):
                return part_grad.at[at_col(zs[d], y if which is A else y_pair), chunk(j)]

            def slot(side, which, j=j):
                return z_full.at[side, 0 if which is A else 1, chunk(j)]

            def halves(side, j=j):
                return z_half.at[side, chunk(j)]

            for k in range(1, 4):
                tasks[f"p{k}{j}"] = lambda k=k, j=j: q_add(k, j)
        p_rings.append(Scatter(f"pz{j}", "z", part, slot, halves))
        for k in range(4):
            lands[f"s{k}{j}"] = q_in.at[k, :, chunk(j)]
            tasks[f"b{k}{j}"] = lambda k=k, j=j: backward(k, j)
        lands[f"fy{j}"] = fy_in.at[chunk(j)]
        tasks[f"fy{j}"] = lambda j=j: pair_end(j)

    def turn(k, y_, needs):
        wait(*needs)
        z_ = hid_z[k]
        rows = pl.ds(pl.multiple_of(y_ * tokens, tokens), tokens)
        for u in range(0, mine, 128):
            width = min(128, mine - u)
            tile = hid[at_col(z_, y_), u : u + width].astype(F32).T
            hid_set[k, rows, u : u + width] = tile.astype(BF16)

    for k, (first, second) in enumerate(arrivals):
        for what, y_, needs in (
            ("a", y, first), ("b", y_pair, second),
            ("c", y_q, (f"h{k}A",)), ("d", 3 - y_pair, (f"h{k}B",)),
        ):
            tasks[f"t{k}{what}"] = lambda args=(k, y_, needs): turn(*args)

    def forward(e, s, k, z_):
        chips, i, where = pl.ds(z_ * 2, 2), 0 if e == "0" else 1, columns_of[e]
        name = f"f{e}{s}"
        if i:
            wait(*[f"w{j}{e}" for j in range(CHUNKS)])
        elif "weight" not in awaited:
            awaited.add("weight")
            load_weight.wait()
        own = pl.ds(pl.multiple_of(kind * mine, 16), mine)

        def step(n, carry):
            columns = pl.ds(pl.multiple_of(where.start + n * 256, 256), 256)
            right = weight_in[:, columns] if i else weight[own, columns]
            product = jnp.dot(hid_set[k], right, preferred_element_type=F32).astype(BF16)
            for b in range(4):
                part_out[i, b % 2, z_ * 2 + b // 2, :, columns] = product[b * tokens : (b + 1) * tokens]
            return carry

        lax.fori_loop(0, where.size // 256, step, 0)
        lands[name] = from_sib.at[i, chips, :, where]
        send(name, part_out.at[i, 1 - core, chips, :, where], from_sib.at[i, chips, :, where], "sib")

    def add_sibling(e, s, z_):
        chips, i, where = pl.ds(z_ * 2, 2), 0 if e == "0" else 1, columns_of[e]
        wait(f"f{e}{s}")
        two = part_out.at[i, core, chips, :, where]
        sum_to(two, (two, from_sib.at[i, chips, :, where]))

    o_zl = (z // 2, 1 - z // 2)

    def o_start(ring):
        ring.far()
        ring.near()

    def o_here(e, m, ring):
        i, where = 0 if e == "0" else 1, columns_of[e]
        ring.wait_all()
        sum_to(
            x_sum.at[i, o_zl[m], :, where],
            (ring.part(0, ALL), x_full.at[i, m, 0, :, where], x_full.at[i, m, 1, :, where]),
        )

    def o_pair(e, m):
        where = columns_of[e]
        send(f"oy{e}{m}", x_sum.at[1, o_zl[m], :, where], pair_in.at[o_zl[m], :, where], "pr")

    def o_cross(e):
        where = columns_of[e]
        wait(f"oy{e}0", f"oy{e}1")
        away = x_sum.at[0, 1 - zl, :, where]
        sum_to(away, (away, pair_in.at[1 - zl, :, where]))
        send(f"oz{e}", away, zl_in.at[:, where], "zl")

    for e, where in columns_of.items():
        i = 0 if e == "0" else 1
        for k, (name, z_) in enumerate(zip("0PO3", hid_z)):
            tasks[f"f{e}{name}"] = lambda args=(e, name, k, z_): forward(*args)
            tasks[f"op{e}{name}"] = lambda args=(e, name, z_): add_sibling(*args)
        for m in range(2):
            ring = Scatter(
                f"o{e}{m}", "x",
                lambda d, rows, i=i, zl_=o_zl[m], where=where: part_out.at[i, core, zl_ * 4 + xs[d], rows, where],
                lambda side, rows, i=i, m=m, where=where: x_full.at[i, m, side, rows, where],
                lambda side, i=i, m=m, where=where: x_half.at[i, m, side, :, where],
            )
            tasks[f"o{e}{m}.start"] = lambda ring=ring: o_start(ring)
            tasks[f"o{e}{m}.here"] = lambda args=(e, m, ring): o_here(*args)
            if i:
                lands[f"oy{e}{m}"] = pair_in.at[o_zl[m], :, where]
                tasks[f"oy{e}{m}"] = lambda args=(e, m): o_pair(*args)
        if i:
            lands[f"oz{e}"] = zl_in.at[:, where]
            tasks[f"oz{e}"] = lambda e=e: o_cross(e)

    @task
    def oend():
        wait("oza", "ozb")
        sum_to(out, (x_sum.at[0, zl], pair_in.at[zl], zl_in))

    @task
    def fin():
        wait(*[f"fy{j}" for j in range(CHUNKS)])
        others = pl.multiple_of((1 - kind) * mine, 16)

        grad_t[pl.ds(others, mine)] = fy_in[...].astype(F32)
        for u in range(0, units, 128):
            grad[:, u : u + 128] = grad_t[pl.ds(u, 128)].T

    barrier = pltpu.get_barrier_semaphore()
    for to in near.values():
        pl.semaphore_signal(barrier, inc=1, device_id=to, device_id_type=pl.DeviceIdType.MESH)
    load_cot = pltpu.make_async_copy(cot, cots.at[0, row], load_sems.at[0])
    load_cot.start()
    load_gate = pltpu.make_async_copy(gate_hbm, gate, load_sems.at[2])
    load_gate.start()
    load_up = pltpu.make_async_copy(up_hbm, up, load_sems.at[3])
    load_up.start()
    load_weight = pltpu.make_async_copy(weight_hbm, weight, load_sems.at[1])
    load_weight.start()
    load_cot.wait()
    pl.semaphore_wait(barrier, len(near))

    steps = list(tasks.values())
    for number in ORDER:
        steps[number]()
    for one in sent:
        one.wait_send()


def finish(gate, up, grad, summed, out, gate_grad, up_grad):
    value = gate[...].astype(F32)
    sigma = 1.0 / (1.0 + jnp.exp(-value))
    scaled = grad[...] * sigma
    gate_grad[...] = (scaled * up[...].astype(F32) * (1.0 + value * (1.0 - sigma))).astype(BF16)
    up_grad[...] = (scaled * value).astype(BF16)
    out[...] = summed[...]


def local(gate_pre, up_pre, down_weight, out_grad):
    tokens, units = gate_pre.shape
    feats = out_grad.shape[1]
    half, mine = tokens // 2, units // 2

    def vmem(*shape):
        return pltpu.VMEM(shape, BF16)

    whole = pl.BlockSpec(memory_space=pltpu.VMEM)
    outside = pl.BlockSpec(memory_space=pl.ANY)
    summed, grad = pl.pallas_call(
        kernel,
        out_shape=(
            jax.ShapeDtypeStruct((tokens, feats), BF16),
            jax.ShapeDtypeStruct((tokens, units), F32),
        ),
        in_specs=[outside] * 4,
        out_specs=(whole,) * 2,
        scratch_shapes=[
            vmem(tokens, units),
            vmem(tokens, units),
            vmem(units, feats),
            vmem(mine, feats),
            vmem(units, tokens),
            vmem(16, mine, tokens),
            vmem(4, 4 * tokens, mine),
            vmem(2, 16, tokens, feats),
            vmem(2, 2, 8, tokens, feats),
            vmem(2, 8, tokens, feats),
            vmem(2, 2, 2, tokens, feats),
            vmem(2, 2, 2, half, feats),
            vmem(2, 2, tokens, feats),
            vmem(2, tokens, feats),
            vmem(tokens, feats),
            vmem(16, mine, tokens),
            vmem(4, 2, mine, tokens),
            vmem(2, 2, mine, tokens),
            vmem(2, mine, tokens),
            vmem(2, 4, mine // CHUNKS, tokens),
            vmem(2, 2, mine // CHUNKS, tokens),
            vmem(mine, tokens),
            vmem(mine, tokens),
            pltpu.VMEM((units, tokens), F32),
            pltpu.SemaphoreType.DMA((SEMAPHORES,)),
            pltpu.SemaphoreType.DMA((SEMAPHORES,)),
            pltpu.SemaphoreType.DMA((4,)),
        ],
        compiler_params=pltpu.CompilerParams(
            collective_id=0, has_side_effects=True, vmem_limit_bytes=60 * 1024 * 1024
        ),
        cost_estimate=pl.CostEstimate(
            flops=4 * 16 * tokens * units * feats, bytes_accessed=8 * 1024 * 1024, transcendentals=0
        ),
    )(gate_pre, up_pre, down_weight, out_grad)
    by_units, by_feats = (pl.BlockSpec((tokens // 2, n), lambda i: (i, 0)) for n in (units, feats))
    return pl.pallas_call(
        finish,
        grid=(2,),
        out_shape=(
            jax.ShapeDtypeStruct((tokens, feats), BF16),
            jax.ShapeDtypeStruct((tokens, units), BF16),
            jax.ShapeDtypeStruct((tokens, units), BF16),
        ),
        in_specs=[by_units, by_units, by_units, by_feats],
        out_specs=(by_feats, by_units, by_units),
    )(gate_pre, up_pre, grad, summed)


def solution(mesh):
    return jax.shard_map(
        local,
        mesh=mesh,
        in_specs=(P("col", "row"), P("col", "row"), P("row", "col"), P("row", "col")),
        out_specs=(P("row", "col"), P("col", "row"), P("col", "row")),
        check_vma=False,
    )
```

time: 368 us -> 104 us (0.28)
  waiting for transfers between devices: 325 us -> 0 us
  Pallas kernels: 0 us -> 104 us
  matrix products: 22.6 us -> 0 us
  between operations: 13.8 us -> 0.64 us
    reduce_scatter x2 -> x0, waiting for transfers between devices: 185 us -> none  [the longest x1 112 us: local(): lax.psum_scatter(partial_grad.astype(jnp.bfloat16), 'col', scatter_dimens...]
    all_gather x2 -> x0, waiting for transfers between devices: 140 us -> none  [the longest x1 94 us: local(): lax.all_gather(hidden_of(gate_pre, up_pre), 'col', axis=0, tiled=True)]
    pallas_call x0 -> x2, Pallas kernels: none -> 104 us  [the longest x1 101 us: local(): pl.pallas_call(kernel, out_shape=(jax.ShapeDtypeStruct((tokens, feats), B...]
    dot_general x2 -> x0, matrix products: 22.6 us -> none  [the longest x1 11.4 us: local(): lax.dot_general(lax.all_gather(out_grad, 'row', axis=0, tiled=True), down...]
  transfers between devices with their start and end apart: 4 -> 0, of which waited for: 4 -> 0; matrix products, arithmetic and copies ran while one was open for 0% -> 0% of each run, Pallas kernels for 0% -> 0%
where the time goes in v4:
time: 104 us
  Pallas kernels  104 us (100%)
    pallas_call x1, Pallas kernels, local(): pl.pallas_call(kernel, out_shape=(jax.ShapeDtypeStruct((tokens, feats), B...  101 us
    pallas_call x1, Pallas kernels, local(): pl.pallas_call(finish, grid=(2,), out_shape=(jax.ShapeDtypeStruct((tokens...  2.54 us

profile of v4, /device:TPU:1, one launch (start us, length us, event | category | flops | bytes accessed | tf_op | source)
XLA Modules:
  0.0 104.2 jit_solution(18260236621890726018)
XLA Ops:
  0.6 101.0 %shard_map.67 = (bf16[128,1024]{1,0:T(8,128)(2,1)}, f32[128,1664]{1,0:T(8,128)}) custom-call(bf16[128,1664]{1,0:T(8,128)(2,1)} %gate.1, bf16[128,1664]{1,0:T(8,128)(2,1)} %up.1, bf16[1664,1024]{1,0:T(8,128)(2,1)} %weight_hbm.1, bf16[128,1024]{1,0:T(8,128)(2,1)} %cot.1), custom_call_target="tpu_custom_call" | custom-call | flops 13958643712 | bytes 8388608 | tf_op jit(solution)/shard_map/pallas_call | solution.py:557
  101.6 2.5 %shard_map.68 = (bf16[128,1024]{1,0:T(8,128)(2,1)}, bf16[128,1664]{1,0:T(8,128)(2,1)}, bf16[128,1664]{1,0:T(8,128)(2,1)}) custom-call(bf16[128,1664]{1,0:T(8,128)(2,1)} %gate.1, bf16[128,1664]{1,0:T(8,128)(2,1)} %up.1, f32[128,1664]{1,0:T(8,128)} %get-tuple-element.5.grad, bf16[128,1024]{1,0:T(8,128)(2,1)} %get-tuple-element.6.summed), custom_call_target="tpu_custom_call" | custom-call | tf_op jit(solution)/shard_map/pallas_call | solution.py:602

commit v5 on v4

--- a/solution.py
+++ b/solution.py
@@ -7,27 +7,30 @@
 
 BF16, F32 = jnp.bfloat16, jnp.float32
 
-CHUNKS = 4
+CHUNKS = (144,176,176,176,160)
 Z_FIRST = (0,)
 
 ORDER = [
-    10, 12, 18, 0, 1, 39, 14, 41, 13, 24, 16, 11,
-    42, 40, 5, 101, 30, 15, 45, 102, 36, 25, 43,
-    37, 9, 3, 32, 99, 44, 22, 17, 20, 100, 26, 7,
-    103, 46, 38, 104, 19, 27, 115, 31, 107, 28,
-    116, 2, 21, 8, 108, 105, 106, 117, 34, 6, 47,
-    111, 109, 23, 35, 33, 164, 29, 162, 118, 128,
-    110, 48, 119, 58, 50, 112, 165, 166, 57, 51,
-    113, 163, 175, 56, 127, 4, 52, 126, 97, 96,
-    114, 168, 173, 167, 174, 121, 53, 54, 169,
-    183, 84, 95, 82, 120, 88, 122, 135, 89, 87,
-    139, 137, 182, 90, 75, 76, 181, 141, 71, 143,
-    86, 91, 140, 138, 150, 83, 73, 93, 70, 92,
-    144, 129, 62, 142, 158, 63, 69, 184, 185, 78,
-    149, 176, 148, 177, 74, 79, 77, 55, 49, 156,
-    80, 94, 157, 133, 68, 134, 61, 60, 66, 151,
-    152, 67, 159, 160, 64, 65, 81, 98, 59, 136,
-    186, 72, 161, 85, 188, 187,
+    12, 14, 20, 0, 1, 43, 41, 15, 16, 114, 13, 32,
+    44, 42, 26, 7, 19, 5, 47, 45, 117, 38, 28, 23,
+    39, 22, 27, 21, 116, 11, 122, 46, 124, 18, 34,
+    9, 33, 40, 115, 48, 3, 36, 202, 180, 29, 118,
+    2, 203, 119, 120, 10, 8, 17, 4, 24, 31, 6,
+    181, 123, 35, 30, 121, 204, 182, 25, 49, 205,
+    215, 126, 183, 193, 37, 157, 155, 50, 125,
+    159, 206, 60, 52, 214, 158, 59, 53, 128, 184,
+    112, 207, 156, 168, 213, 127, 58, 54, 111,
+    160, 129, 161, 99, 103, 104, 110, 56, 55, 208,
+    167, 166, 162, 176, 73, 102, 105, 98, 97, 90,
+    91, 107, 71, 209, 222, 101, 106, 130, 132,
+    174, 175, 108, 64, 65, 134, 136, 86, 131, 133,
+    143, 89, 88, 93, 92, 72, 135, 95, 137, 151,
+    94, 169, 85, 170, 62, 186, 77, 78, 141, 142,
+    220, 84, 177, 221, 69, 178, 63, 66, 96, 68,
+    149, 67, 150, 57, 51, 144, 145, 185, 187, 200,
+    191, 76, 75, 80, 81, 79, 70, 152, 153, 192,
+    82, 83, 223, 216, 198, 199, 100, 179, 109, 74,
+    194, 61, 201, 154, 87, 113, 225, 224,
 ]
 SEMAPHORES = 256
 
@@ -42,7 +45,6 @@
     tokens, units = gate.shape
     feats = weight.shape[1]
     half, mine = tokens // 2, units // 2
-    step_rows = mine // CHUNKS
     A, B, ALL = pl.ds(0, half), pl.ds(half, half), pl.ds(0, tokens)
 
     row, col = lax.axis_index("row"), lax.axis_index("col")
@@ -224,18 +226,18 @@
     lands["e0"] = hid.at[at_col(z, y_pair)]
 
     def chunk(j):
-        return pl.ds(j * step_rows, step_rows)
-
-    columns_of = {"0": pl.ds(0, feats), "a": pl.ds(0, feats // 2), "b": pl.ds(feats // 2, feats // 2)}
+        return pl.ds(sum(CHUNKS[:j]), CHUNKS[j])
+
+    columns_of = {e: pl.ds(n % 2 * (feats // 2), feats // 2) for n, e in enumerate("abcd")}
 
     def w_send(j, e):
         if "weight" not in awaited:
             awaited.add("weight")
             load_weight.wait()
-        rows = pl.ds(pl.multiple_of((1 - kind) * mine + j * step_rows, 16), step_rows)
+        rows = pl.ds(pl.multiple_of((1 - kind) * mine + sum(CHUNKS[:j]), 16), CHUNKS[j])
         send(f"w{j}{e}", weight.at[rows, columns_of[e]], weight_in.at[chunk(j), columns_of[e]], "pr")
 
-    for j in range(CHUNKS):
+    for j in range(len(CHUNKS)):
         for e in "ab":
             lands[f"w{j}{e}"] = weight_in.at[chunk(j), columns_of[e]]
             tasks[f"w{j}{e}"] = lambda j=j, e=e: w_send(j, e)
@@ -334,7 +336,7 @@
             awaited.add("weight")
             load_weight.wait()
         four = pl.ds(set_z[k] * 4, 4)
-        own = pl.ds(pl.multiple_of(kind * mine + j * step_rows, 16), step_rows)
+        own = pl.ds(pl.multiple_of(kind * mine + sum(CHUNKS[:j]), 16), CHUNKS[j])
         total = None
         for i, rows in enumerate((weight[own], weight_in[chunk(j)])):
             right = cots[i, four].reshape(4 * tokens, feats)
@@ -356,10 +358,10 @@
         p_rings[j].wait_all()
         sides = () if j in Z_FIRST else (0, 1)
         own, others = at_col(z, y), at_col(z, y_pair)
-        to = pl.multiple_of(kind * mine + j * step_rows, 16)
-
-        for i in range(step_rows // 16):
-            rows = pl.ds(j * step_rows + i * 16, 16)
+        to = pl.multiple_of(kind * mine + sum(CHUNKS[:j]), 16)
+
+        for i in range(CHUNKS[j] // 16):
+            rows = pl.ds(sum(CHUNKS[:j]) + i * 16, 16)
             fy_out[rows] = total_of(
                 [part_grad[others, rows], q_in[0, 1 - y % 2, rows]] + [z_full[side, 1, rows] for side in sides]
             ).astype(BF16)
@@ -377,7 +379,7 @@
                 q_send(0, j)
 
     p_rings = []
-    for j in range(CHUNKS):
+    for j in range(len(CHUNKS)):
         if j in Z_FIRST:
 
             def part(d, which, j=j):
@@ -427,29 +429,24 @@
             tasks[f"t{k}{what}"] = lambda args=(k, y_, needs): turn(*args)
 
     def forward(e, s, k, z_):
-        chips, i, where = pl.ds(z_ * 2, 2), 0 if e == "0" else 1, columns_of[e]
+        chips, i, where = pl.ds(z_ * 2, 2), 1 if e in "ab" else 0, columns_of[e]
         name = f"f{e}{s}"
         if i:
-            wait(*[f"w{j}{e}" for j in range(CHUNKS)])
+            wait(*[f"w{j}{e}" for j in range(len(CHUNKS))])
         elif "weight" not in awaited:
             awaited.add("weight")
             load_weight.wait()
         own = pl.ds(pl.multiple_of(kind * mine, 16), mine)
 
-        def step(n, carry):
-            columns = pl.ds(pl.multiple_of(where.start + n * 256, 256), 256)
-            right = weight_in[:, columns] if i else weight[own, columns]
-            product = jnp.dot(hid_set[k], right, preferred_element_type=F32).astype(BF16)
-            for b in range(4):
-                part_out[i, b % 2, z_ * 2 + b // 2, :, columns] = product[b * tokens : (b + 1) * tokens]
-            return carry
-
-        lax.fori_loop(0, where.size // 256, step, 0)
+        right = weight_in[:, where] if i else weight[own, where]
+        product = jnp.dot(hid_set[k], right, preferred_element_type=F32).astype(BF16)
+        for b in range(4):
+            part_out[i, b % 2, z_ * 2 + b // 2, :, where] = product[b * tokens : (b + 1) * tokens]
         lands[name] = from_sib.at[i, chips, :, where]
         send(name, part_out.at[i, 1 - core, chips, :, where], from_sib.at[i, chips, :, where], "sib")
 
     def add_sibling(e, s, z_):
-        chips, i, where = pl.ds(z_ * 2, 2), 0 if e == "0" else 1, columns_of[e]
+        chips, i, where = pl.ds(z_ * 2, 2), 1 if e in "ab" else 0, columns_of[e]
         wait(f"f{e}{s}")
         two = part_out.at[i, core, chips, :, where]
         sum_to(two, (two, from_sib.at[i, chips, :, where]))
@@ -461,7 +458,7 @@
         ring.near()
 
     def o_here(e, m, ring):
-        i, where = 0 if e == "0" else 1, columns_of[e]
+        i, where = 1 if e in "ab" else 0, columns_of[e]
         ring.wait_all()
         sum_to(
             x_sum.at[i, o_zl[m], :, where],
@@ -480,7 +477,7 @@
         send(f"oz{e}", away, zl_in.at[:, where], "zl")
 
     for e, where in columns_of.items():
-        i = 0 if e == "0" else 1
+        i = 1 if e in "ab" else 0
         for k, (name, z_) in enumerate(zip("0PO3", hid_z)):
             tasks[f"f{e}{name}"] = lambda args=(e, name, k, z_): forward(*args)
             tasks[f"op{e}{name}"] = lambda args=(e, name, z_): add_sibling(*args)
@@ -507,7 +504,7 @@
 
     @task
     def fin():
-        wait(*[f"fy{j}" for j in range(CHUNKS)])
+        wait(*[f"fy{j}" for j in range(len(CHUNKS))])
         others = pl.multiple_of((1 - kind) * mine, 16)
 
         grad_t[pl.ds(others, mine)] = fy_in[...].astype(F32)
@@ -582,8 +579,8 @@
             vmem(4, 2, mine, tokens),
             vmem(2, 2, mine, tokens),
             vmem(2, mine, tokens),
-            vmem(2, 4, mine // CHUNKS, tokens),
-            vmem(2, 2, mine // CHUNKS, tokens),
+            vmem(2, 4, sum(CHUNKS[j] for j in Z_FIRST), tokens),
+            vmem(2, 2, sum(CHUNKS[j] for j in Z_FIRST), tokens),
             vmem(mine, tokens),
             vmem(mine, tokens),
             pltpu.VMEM((units, tokens), F32),

time: 104 us -> 103 us (level)
  Pallas kernels: 104 us -> 102 us
    pallas_call x1, Pallas kernels: 101 us -> 99.5 us  [local(): pl.pallas_call(kernel, out_shape=(jax.ShapeDtypeStruct((tokens, feats), B...]
where the time goes in v5:
time: 103 us
  Pallas kernels  102 us (99%)
    pallas_call x1, Pallas kernels, local(): pl.pallas_call(kernel, out_shape=(jax.ShapeDtypeStruct((tokens, feats), B...  99.5 us
    pallas_call x1, Pallas kernels, local(): pl.pallas_call(finish, grid=(2,), out_shape=(jax.ShapeDtypeStruct((tokens...  2.54 us

profile of v5, /device:TPU:1, one launch (start us, length us, event | category | flops | bytes accessed | tf_op | source)
XLA Modules:
  0.0 102.7 jit_solution(8398462947893820003)
XLA Ops:
  0.6 99.5 %shard_map.67 = (bf16[128,1024]{1,0:T(8,128)(2,1)}, f32[128,1664]{1,0:T(8,128)}) custom-call(bf16[128,1664]{1,0:T(8,128)(2,1)} %gate.1, bf16[128,1664]{1,0:T(8,128)(2,1)} %up.1, bf16[1664,1024]{1,0:T(8,128)(2,1)} %weight_hbm.1, bf16[128,1024]{1,0:T(8,128)(2,1)} %cot.1), custom_call_target="tpu_custom_call" | custom-call | flops 13958643712 | bytes 8388608 | tf_op jit(solution)/shard_map/pallas_call | solution.py:554
  100.1 2.5 %shard_map.68 = (bf16[128,1024]{1,0:T(8,128)(2,1)}, bf16[128,1664]{1,0:T(8,128)(2,1)}, bf16[128,1664]{1,0:T(8,128)(2,1)}) custom-call(bf16[128,1664]{1,0:T(8,128)(2,1)} %gate.1, bf16[128,1664]{1,0:T(8,128)(2,1)} %up.1, f32[128,1664]{1,0:T(8,128)} %get-tuple-element.5.grad, bf16[128,1024]{1,0:T(8,128)(2,1)} %get-tuple-element.6.summed), custom_call_target="tpu_custom_call" | custom-call | tf_op jit(solution)/shard_map/pallas_call | solution.py:599

commit v6 on v5

--- a/solution.py
+++ b/solution.py
@@ -33,6 +33,7 @@
     194, 61, 201, 154, 87, 113, 225, 224,
 ]
 SEMAPHORES = 256
+PATIENCE = {"sib": 12, "xp": 40, "xm": 40, "q": 50, "zp": 60, "zm": 60, "zl": 60, "pr": 140}
 
 
 def kernel(
@@ -74,6 +75,7 @@
     }
 
     numbers, awaited, sent, lands, tasks = {}, set(), [], {}, {}
+    counter = [0]
 
     def copy(name, src, dst, to):
         number = numbers.setdefault(name, len(numbers))
@@ -89,7 +91,8 @@
     def send(name, src, dst, to):
         one = copy(name, src, dst, to)
         one.start()
-        sent.append(one)
+        sent.append((one, counter[0] + PATIENCE[to]))
+        counter[0] += 1
 
     def wait(*names):
         for name in names:
@@ -528,7 +531,11 @@
     steps = list(tasks.values())
     for number in ORDER:
         steps[number]()
-    for one in sent:
+        for one, due in sent:
+            if due <= counter[0]:
+                one.wait_send()
+        sent[:] = [entry for entry in sent if entry[1] > counter[0]]
+    for one, _ in sent:
         one.wait_send()
 
 

time: 103 us -> 103 us (level)
  no operation moved by 1% of the time
where the time goes in v6:
time: 103 us; the launch traced here: 102 us
  Pallas kernels  101 us (98%)
    pallas_call x1, Pallas kernels, local(): pl.pallas_call(kernel, out_shape=(jax.ShapeDtypeStruct((tokens, feats), B...  98.9 us
    pallas_call x1, Pallas kernels, local(): pl.pallas_call(finish, grid=(2,), out_shape=(jax.ShapeDtypeStruct((tokens...  2.54 us

profile of v6, /device:TPU:1, one launch (start us, length us, event | category | flops | bytes accessed | tf_op | source)
XLA Modules:
  0.0 102.1 jit_solution(18186836662885208507)
XLA Ops:
  0.6 98.9 %shard_map.67 = (bf16[128,1024]{1,0:T(8,128)(2,1)}, f32[128,1664]{1,0:T(8,128)}) custom-call(bf16[128,1664]{1,0:T(8,128)(2,1)} %gate.1, bf16[128,1664]{1,0:T(8,128)(2,1)} %up.1, bf16[1664,1024]{1,0:T(8,128)(2,1)} %weight_hbm.1, bf16[128,1024]{1,0:T(8,128)(2,1)} %cot.1), custom_call_target="tpu_custom_call" | custom-call | flops 13958643712 | bytes 8388608 | tf_op jit(solution)/shard_map/pallas_call | solution.py:561
  99.5 2.5 %shard_map.68 = (bf16[128,1024]{1,0:T(8,128)(2,1)}, bf16[128,1664]{1,0:T(8,128)(2,1)}, bf16[128,1664]{1,0:T(8,128)(2,1)}) custom-call(bf16[128,1664]{1,0:T(8,128)(2,1)} %gate.1, bf16[128,1664]{1,0:T(8,128)(2,1)} %up.1, f32[128,1664]{1,0:T(8,128)} %get-tuple-element.5.grad, bf16[128,1024]{1,0:T(8,128)(2,1)} %get-tuple-element.6.summed), custom_call_target="tpu_custom_call" | custom-call | tf_op jit(solution)/shard_map/pallas_call | solution.py:606
